TPU v7x, 32 devices: a whole 2x2x4 slice. The times are simulated.
32 devices in a mesh: ctx: 16 (over z, y, x), grp: 2 (over core).
Axes of the slice: x: 2, y: 2, z: 4, core: 2. Of those that a mesh axis runs over, the one named last changes fastest.
Arguments:
- tokens: bfloat16 [8192, 4096], P('ctx'), may hold values from -6 to 6
- w_z: bfloat16 [4096, 8192], P('ctx', 'grp'), may hold values from -0.09375 to 0.09375
- w_x: bfloat16 [4096, 8192], P('ctx', 'grp'), may hold values from -0.09375 to 0.09375
- w_bc: bfloat16 [4096, 8, 256], P('ctx', 'grp'), may hold values from -0.09375 to 0.09375
- w_dt: bfloat16 [4096, 128], P('ctx', 'grp'), may hold values from -0.09375 to 0.09375
- conv_x: float32 [4, 8192], P(None, 'grp'), may hold values from -3 to 3
- conv_bc: float32 [4, 8, 256], P(None, 'grp'), may hold values from -3 to 3
- bias_x: float32 [8192], P('grp'), may hold values from -3 to 3
- bias_bc: float32 [8, 256], P('grp'), may hold values from -3 to 3
- dt_bias: float32 [128], P('grp'), may hold values from -5.3 to -3
- a_log: float32 [128], P('grp'), as said below
- d_skip: float32 [128], P('grp'), may hold values from 0.5 to 1.5
- norm_gain: float32 [8192], P('grp'), may hold values from 0.5 to 1.5
Outputs:
- layer_out: bfloat16 [8192, 8192], P('ctx', 'grp')
Inputs may be any that keep to these rules, and one draw needn't show every extreme that they name: `a_log`: each head's log decay rate; some heads forget within tens of tokens, others keep much of their state over all 8192 tokens.
All inputs are finite; a program needn't handle non-finite values.
Results may differ from a plain program's by a relative error of at most 0.013.
Values may be sent and summed in bfloat16 or wider, within the bound.
A program may use at most 192 MiB of HBM per device.

v0:
```python
import jax
import jax.numpy as jnp
from jax import lax
from jax.sharding import PartitionSpec as P

SPAN = 256


def shifted(value, axis, steps):
    count = lax.axis_size(axis)
    leading, last = (max(0, -steps), min(count, count - steps))
    return lax.ppermute(value, axis, [(source, source + steps) for source in range(leading, last)])


def prefix(value, axis, combine, identity):
    devices, mine = (lax.axis_size(axis), lax.axis_index(axis))
    everything = jax.tree.map(
        lambda part, kind: lax.all_gather(part.astype(kind), axis),
        value,
        (jnp.bfloat16, jnp.bfloat16),
    )
    start = jax.tree.map(
        lambda part, zero: jnp.broadcast_to(jnp.asarray(zero, part.dtype), part.shape),
        value,
        identity,
    )

    def turn(k, before):
        reached = k < mine
        new = combine(
            before, jax.tree.map(lambda part, own: part[k].astype(own.dtype), everything, value)
        )
        return jax.tree.map(lambda a, b: jnp.where(reached, a, b), new, before)

    return lax.fori_loop(0, devices, turn, start)


def make_folder(source, pieces):
    piece_rows = pieces[0].shape[0]
    return tuple(
        (
            jnp.dot(source, piece.reshape(piece_rows, -1), preferred_element_type=jnp.float32)
            for piece in pieces
        )
    )


def causal_taps(extended, taps, offset_bias, tok_rows, kernel):
    running = jnp.zeros((tok_rows, taps.shape[1]), jnp.float32) + offset_bias[None, :]
    for tap in range(kernel):
        running = running + taps[tap][None, :] * extended[tap : tap + tok_rows].astype(jnp.float32)
    return jax.nn.silu(running).astype(jnp.bfloat16)


def combine_states(earlier, later):
    return (earlier[0] + later[0], jnp.exp(later[0])[:, None, None] * earlier[1] + later[1])


def on_device(
    tokens,
    w_z,
    w_x,
    w_bc,
    w_dt,
    conv_x,
    conv_bc,
    bias_x,
    bias_bc,
    dt_bias,
    a_log,
    d_skip,
    norm_gain,
):
    tok_rows = tokens.shape[0]
    kernel = conv_x.shape[0]
    inner_width = conv_x.shape[1]
    group_count = w_bc.shape[1]
    state_size = w_bc.shape[2] // 2
    bc_width = group_count * 2 * state_size
    head_count = w_dt.shape[1]
    head_dim = inner_width // head_count
    per_group = head_count // group_count
    span_len = SPAN
    blocks = tok_rows // span_len
    gate_sum, inner_sum, mix_sum, step_sum = make_folder(
        tokens,
        (
            lax.all_gather(w_z, "ctx", axis=0, tiled=True),
            lax.all_gather(w_x, "ctx", axis=0, tiled=True),
            lax.all_gather(w_bc, "ctx", axis=0, tiled=True),
            lax.all_gather(w_dt, "ctx", axis=0, tiled=True),
        ),
    )
    gate_rows = gate_sum.astype(jnp.bfloat16)
    inner = inner_sum.astype(jnp.bfloat16)
    mixed = mix_sum.astype(jnp.bfloat16)
    inner_edge, mixed_edge = shifted(
        (inner[tok_rows - (kernel - 1) :], mixed[tok_rows - (kernel - 1) :]), "ctx", 1
    )
    inner_ext = jnp.concatenate([inner_edge, inner], axis=0)
    mixed_ext = jnp.concatenate([mixed_edge, mixed], axis=0)
    inner_c = causal_taps(inner_ext, conv_x, bias_x, tok_rows, kernel)
    mix_c = causal_taps(
        mixed_ext, conv_bc.reshape(kernel, bc_width), bias_bc.reshape(bc_width), tok_rows, kernel
    )
    mix_c = mix_c.reshape(blocks, span_len, group_count, 2 * state_size)
    b_in = mix_c[..., :state_size]
    c_in = mix_c[..., state_size:]
    inner_in = inner_c.reshape(blocks, span_len, head_count, head_dim)
    step_size = jax.nn.softplus(step_sum + dt_bias[None, :])
    log_rate = -jnp.exp(a_log)[None, :] * step_size
    cumul = jnp.cumsum(log_rate.reshape(blocks, span_len, head_count), axis=1)
    step_block = step_size.reshape(blocks, span_len, head_count)
    scores = jnp.einsum("cign,cjgn->cgij", c_in, b_in, preferred_element_type=jnp.float32)
    scores_h = jnp.broadcast_to(
        scores[:, :, None], (blocks, group_count, per_group, span_len, span_len)
    )
    scores_h = scores_h.reshape(blocks, head_count, span_len, span_len)
    cumul_t = jnp.swapaxes(cumul, 1, 2)
    log_gap = cumul_t[:, :, :, None] - cumul_t[:, :, None, :]
    causal_mask = jnp.arange(span_len)[:, None] >= jnp.arange(span_len)[None, :]
    decay_mat = jnp.where(causal_mask[None, None], jnp.exp(jnp.minimum(log_gap, 0.0)), 0.0)
    step_t = jnp.swapaxes(step_block, 1, 2)
    weight = (scores_h * decay_mat * step_t[:, :, None, :]).astype(jnp.bfloat16)
    intra = jnp.einsum("chij,cjhp->cihp", weight, inner_in, preferred_element_type=jnp.float32)
    block_log = cumul[:, -1, :]
    b_heads = jnp.broadcast_to(
        b_in[:, :, :, None], (blocks, span_len, group_count, per_group, state_size)
    )
    b_heads = b_heads.reshape(blocks, span_len, head_count, state_size).astype(jnp.float32)
    weighted_b = (
        (jnp.exp(block_log[:, None, :] - cumul) * step_block)[..., None] * b_heads
    ).astype(jnp.bfloat16)
    local_state = jnp.einsum(
        "cjhn,cjhp->chnp", weighted_b, inner_in, preferred_element_type=jnp.float32
    )
    zero_state = jnp.zeros((head_count, state_size, head_dim), jnp.float32)
    zero_log = jnp.zeros((head_count,), jnp.float32)
    starts = []
    logs_before = []
    for block in range(blocks):
        starts.append(zero_state)
        logs_before.append(zero_log)
        zero_state = jnp.exp(block_log[block])[:, None, None] * zero_state + local_state[block]
        zero_log = zero_log + block_log[block]
    carried_log, carried = prefix(
        (zero_log, zero_state),
        "ctx",
        combine_states,
        (jnp.zeros_like(zero_log), jnp.zeros_like(zero_state)),
    )
    start_states = jnp.stack(
        [
            jnp.exp(logs_before[block])[:, None, None] * carried + starts[block]
            for block in range(blocks)
        ]
    )
    c_heads = jnp.broadcast_to(
        c_in[:, :, :, None], (blocks, span_len, group_count, per_group, state_size)
    )
    c_heads = c_heads.reshape(blocks, span_len, head_count, state_size).astype(jnp.float32)
    inter = jnp.einsum("cihn,chnp->cihp", c_heads, start_states, precision=lax.Precision.HIGHEST)
    inter = inter * jnp.exp(cumul)[..., None]
    scan_out = intra + inter + d_skip[None, None, :, None] * inner_in.astype(jnp.float32)
    gated = scan_out.reshape(tok_rows, inner_width) * jax.nn.silu(gate_rows.astype(jnp.float32))
    grouped = gated.reshape(tok_rows, group_count, per_group * head_dim)
    scale = lax.rsqrt(jnp.mean(grouped * grouped, axis=-1, keepdims=True) + 1e-05)
    result = (grouped * scale).reshape(tok_rows, inner_width) * norm_gain[None, :]
    return result.astype(jnp.bfloat16)


def solution(mesh):
    placed = (
        P("ctx", None),
        P("ctx", "grp"),
        P("ctx", "grp"),
        P("ctx", "grp", None),
        P("ctx", "grp"),
        P(None, "grp"),
        P(None, "grp", None),
        P("grp"),
        P("grp", None),
        P("grp"),
        P("grp"),
        P("grp"),
        P("grp"),
    )
    return jax.shard_map(
        on_device, mesh=mesh, in_specs=placed, out_specs=P("ctx", "grp"), check_vma=False
    )
```

profile of v0, /device:TPU:27, one launch (start us, length us, event | category | flops | bytes accessed | tf_op | source)
XLA Modules:
  0.0 1175.0 jit_solution(15231321158100227968)
XLA Ops:
  8.7 30.9 %all_gather.22 = bf16[4096,64]{0,1:T(8,128)(2,1)S(1)} all-gather(bf16[256,64]{0,1:T(8,128)(2,1)} %param.19), channel_id=1, replica_groups=mesh['ctx'=16,'grp'=2] {'ctx'}, dimensions={0}, use_global_device_ids=true | all-gather | bytes 557056 | tf_op jit(solution)/shard_map/all_gather | solution.py:91
  46.7 77.4 %all-gather.8.cloned.1.call-done = bf16[4096,4,256]{2,1,0:T(4,128)(2,1)} async-done(((bf16[256,4,256]{2,1,0:T(4,128)(2,1)}), bf16[4096,4,256]{2,1,0:T(4,128)(2,1)}) %all-gather.8.cloned.1.call-update) | async-done | bytes 8388624 | tf_op jit(solution)/shard_map/all_gather | solution.py:90
  124.1 9.6 copy.129
  133.7 7.4 convolution_convert_fusion.2
  148.8 327.2 %all-gather.6.cloned.1.call-done = bf16[4096,4096]{1,0:T(8,128)(2,1)} async-done(((bf16[256,4096]{1,0:T(8,128)(2,1)}), bf16[4096,4096]{1,0:T(8,128)(2,1)}) %all-gather.6.cloned.1.call-update) | async-done | bytes 33554448 | tf_op jit(solution)/shard_map/all_gather | solution.py:89
  476.0 22.6 %convolution_convert_fusion.1 = bf16[512,4096]{1,0:T(8,128)(2,1)S(1)} fusion(bf16[512,4096]{1,0:T(8,128)(2,1)} %param.15, bf16[4096,4096]{1,0:T(8,128)(2,1)} %all-gather.6.cloned.1.call-done), kind=kOutput, calls=%fused_computation.22 | convolution fusion | flops 17181966336 | bytes 41943040 | tf_op jit(solution)/shard_map/dot_general | solution.py:42
  503.3 7.0 multiply_convert_fusion.5
  510.3 12.6 %reshape.167 = bf16[2,256,64,64]{3,2,1,0:T(8,128)(2,1)} reshape(bf16[512,4096]{1,0:T(8,128)(2,1)} %multiply_convert_fusion.5) | data formatting | bytes 8388608 | tf_op jit(solution)/shard_map/reshape | solution.py:109
  522.9 10.5 copy.103
  535.5 8.3 fusion.7
  548.2 25.7 %all-gather = bf16[16,1,64]{2,1,0:T(2,128)(2,1)S(1)} all-gather(bf16[1,1,64]{2,1,0:T(2,128)(2,1)S(1)} %copy.104), channel_id=2, replica_groups=mesh['ctx'=16,'grp'=2] {'ctx'}, dimensions={0}, use_global_device_ids=true | all-gather | bytes 2176 | tf_op jit(solution)/shard_map/all_gather | solution.py:18
  576.7 162.9 %all-gather.10.cloned.1.call-done = bf16[16,64,128,64]{2,3,1,0:T(8,128)(2,1)} async-done(((bf16[1,64,128,64]{2,3,1,0:T(8,128)(2,1)}), bf16[16,64,128,64]{2,3,1,0:T(8,128)(2,1)}) %all-gather.10.cloned.1.call-update) | async-done | bytes 16777232 | tf_op jit(solution)/shard_map/all_gather | solution.py:18
  739.6 122.3 %while.14 = (s32[]{:T(128)}, f32[64,128,64]{2,1,0:T(8,128)}, s32[]{:T(128)}, bf16[16,64]{1,0:T(8,128)(2,1)S(1)}, bf16[16,64,128,64]{2,3,1,0:T(8,128)(2,1)}, /*index=5*/s32[]{:T(128)}, s32[]{:T(128)}) while((s32[]{:T(128)}, f32[64,128,64]{2,1,0:T(8,128)}, s32[]{:T(128)}, bf16[16,64]{1,0:T(8,128)(2,1)S(1)}, ...), condition=%wide.region_3.4_spmd.clone, body=%wide.region_2.3_spmd.clone.sunk | while | flops 2621508 | bytes 9437937 | solution.py:35
  747.5 5.5 fusion.43
  763.3 5.4 fusion.43
  771.1 5.3 fusion.43
  778.8 5.3 fusion.43
  786.6 5.3 fusion.43
  810.0 5.5 fusion.43
  817.9 5.4 fusion.43
  825.7 5.3 fusion.43
  833.4 5.3 fusion.43
  871.4 12.7 %fusion.13 = f32[2,64,64,256]{3,2,1,0:T(8,128)} fusion(bf16[2,256,64,128]{3,1,2,0:T(8,128)(2,1)S(1)} %bitcast.101, f32[1,64,128,64]{2,3,1,0:T(8,128)} %fusion.19, f32[1,64,128,64]{2,3,1,0:T(8,128)} %bitcast.104), kind=kOutput, calls=%fused_computation.28 | convolution fusion | flops 3222274048 | bytes 20971520 | tf_op jit(solution)/shard_map/cihn,chnp->cihp/dot_general | solution.py:162
  884.1 15.3 %broadcast_in_dim.14 = f32[2,4,16,256,256]{4,3,2,1,0:T(8,128)} broadcast(f32[2,4,256,256]{3,2,1,0:T(8,128)} %fusion.22), dimensions={0,1,3,4} | broadcast | bytes 35651584 | tf_op jit(solution)/shard_map/broadcast_in_dim | solution.py:115
  899.5 21.3 %fusion.9 = f32[2,256,64,64]{1,3,2,0:T(8,128)} fusion(f32[2,64,64,256]{3,2,1,0:T(8,128)S(1)} %copy-done.3, bf16[2,256,64,64]{1,3,2,0:T(8,128)(2,1)S(1)} %copy-done.1, f32[64]{0:T(128)S(1)} %copy-done.15, f32[2,256,64]{1,2,0:T(8,128)} %get-tuple-element.164, f32[2,64,256,256]{3,2,1,0:T(8,128)} %bitcast.100, f32[2,64,256]{2,1,0:T(8,128)S(1)} %copy.102, ...), kind=kOutput, calls=%fused_computation.17 | convolution fusion | flops 1134559232 | bytes 54984960 | tf_op jit(solution)/shard_map/chij,cjhp->cihp/dot_general | solution.py:125
  920.8 16.3 %copy.115 = f32[2,256,64,64]{3,2,1,0:T(8,128)} copy(f32[2,256,64,64]{1,3,2,0:T(8,128)} %fusion.9) | data formatting | bytes 16777216 | tf_op jit(solution)/shard_map/reshape | solution.py:165
  937.1 14.8 %reshape.166 = f32[512,4096]{1,0:T(8,128)} reshape(f32[2,256,64,64]{3,2,1,0:T(8,128)} %copy.115) | data formatting | bytes 16777216 | tf_op jit(solution)/shard_map/reshape | solution.py:165
  951.9 139.2 %all-gather.12.cloned.1.call-done = bf16[4096,4096]{1,0:T(8,128)(2,1)} async-done(((bf16[256,4096]{1,0:T(8,128)(2,1)}), bf16[4096,4096]{1,0:T(8,128)(2,1)}) %all-gather.12.cloned.1.call-update) | async-done | bytes 33554448 | tf_op jit(solution)/shard_map/all_gather | solution.py:88
  1091.1 39.4 %fusion.30 = (f32[512,4096]{1,0:T(8,128)}, f32[512,4096]{1,0:T(8,128)}) fusion(f32[512,4096]{1,0:T(8,128)} %reshape.166, bf16[512,4096]{1,0:T(8,128)(2,1)} %param.15, bf16[4096,4096]{1,0:T(8,128)(2,1)} %all-gather.12.cloned.1.call-done), kind=kOutput, calls=%fused_computation.76 | convolution fusion | flops 17196646400 | bytes 62914560 | tf_op jit(solution)/shard_map/dot_general | solution.py:42
  1130.5 10.8 mul.263
  1147.1 11.3 copy.133
  1158.5 9.8 multiply_convert_fusion.4
  (141 shorter events, 119.4 us)
Async XLA Ops:
  6.5 117.6 %all-gather.8.cloned.1.call-start = ((), (), s32[]{:S(2)}) async-start(), calls=%async_computation.1 | async-start | bytes 8912896 | tf_op jit(solution)/shard_map/all_gather | solution.py:90
  7.3 38.0 %copy-start.11 = (f32[4,4,256]{2,1,0:T(4,128)S(1)}, f32[4,4,256]{2,1,0:T(4,128)}, u32[]{:S(2)}) copy-start(f32[4,4,256]{2,1,0:T(4,128)} %param.21) | copy-start | bytes 49156
  7.3 38.7 %copy-start.9 = (f32[4,4096]{1,0:T(4,128)S(1)}, f32[4,4096]{1,0:T(4,128)}, u32[]{:S(2)}) copy-start(f32[4,4096]{1,0:T(4,128)} %param.20) | copy-start | bytes 196612
  7.3 468.7 %all-gather.6.cloned.1.call-start = ((), (), s32[]{:S(2)}) async-start(), calls=%async_computation | async-start | bytes 35651584 | tf_op jit(solution)/shard_map/all_gather | solution.py:89
  8.0 731.6 %all-gather.10.cloned.1.call-start = ((), (), s32[]{:S(2)}) async-start(), calls=%async_computation.2 | async-start | bytes 17825792 | tf_op jit(solution)/shard_map/all_gather | solution.py:18
  124.1 9.6 copy-start.4
  133.7 11.4 copy-start.13
  141.1 4.9 collective-permute-start.1
  148.8 354.5 %copy-start.6 = (f32[1,4096]{1,0:T(1,128)S(1)}, f32[1,4096]{1,0:T(1,128)}, u32[]{:S(2)}) copy-start(f32[1,4096]{1,0:T(1,128)} %get-tuple-element.167) | copy-start | bytes 49156
  148.8 354.5 %copy-start.7 = (f32[1,4096]{1,0:T(1,128)S(1)}, f32[1,4096]{1,0:T(1,128)}, u32[]{:S(2)}) copy-start(f32[1,4096]{1,0:T(1,128)} %get-tuple-element.168) | copy-start | bytes 49156
  148.8 354.5 %copy-start.8 = (f32[1,4096]{1,0:T(1,128)S(1)}, f32[1,4096]{1,0:T(1,128)}, u32[]{:S(2)}) copy-start(f32[1,4096]{1,0:T(1,128)} %get-tuple-element.169) | copy-start | bytes 49156
  148.8 354.5 %copy-start.10 = (f32[4096]{0:T(1024)S(1)}, f32[4096]{0:T(1024)}, u32[]{:S(2)}) copy-start(f32[4096]{0:T(1024)} %param.22) | copy-start | bytes 49156
  498.6 4.7 collective-permute-start
  535.5 10.4 copy-start.14
  543.9 2.1 copy-start
  547.4 543.8 %all-gather.12.cloned.1.call-start = ((), (), s32[]{:S(2)}) async-start(), calls=%async_computation.3 | async-start | bytes 35651584 | tf_op jit(solution)/shard_map/all_gather | solution.py:88
  864.8 1.3 copy-start.2
  866.1 3.3 copy-start.5
  884.1 15.4 %copy-start.1 = (bf16[2,256,64,64]{1,3,2,0:T(8,128)(2,1)S(1)}, bf16[2,256,64,64]{1,3,2,0:T(8,128)(2,1)}, u32[]{:S(2)}) copy-start(bf16[2,256,64,64]{1,3,2,0:T(8,128)(2,1)} %copy.103) | copy-start | bytes 12582916
  884.1 15.4 %copy-start.3 = (f32[2,64,64,256]{3,2,1,0:T(8,128)S(1)}, f32[2,64,64,256]{3,2,1,0:T(8,128)}, u32[]{:S(2)}) copy-start(f32[2,64,64,256]{3,2,1,0:T(8,128)} %fusion.13) | copy-start | bytes 25165828
  884.1 15.4 %copy-start.15 = (f32[64]{0:T(128)S(1)}, f32[64]{0:T(128)}, u32[]{:S(2)}) copy-start(f32[64]{0:T(128)} %param.26) | copy-start | bytes 772
  1147.1 11.4 copy-start.12
Sparse Core Ops, SparseCore 0:
  10.1 113.9 all-gather.7
  126.9 349.0 all-gather.5
  547.5 192.0 all-gather.9
  742.2 348.8 all-gather.11
where the time goes:
time: 1190 us; the launch traced here: 1170 us
  waiting for transfers between devices  711 us (60%)
  local copies, waits for them, and re-layouts  155 us (13%)
  matrix products  117 us (10%)
  other arithmetic  115 us (10%)
  blocking collectives  56.6 us (5%)
  between operations  13.7 us (1%)
    all_gather x1, waiting for transfers between devices, on_device(): lax.all_gather(w_x, 'ctx', axis=0, tiled=True)  327 us
    all_gather x1, waiting for transfers between devices, prefix(): lax.all_gather(part.astype(kind), axis)  163 us
    all_gather x1, waiting for transfers between devices, on_device(): lax.all_gather(w_z, 'ctx', axis=0, tiled=True)  139 us
    select_n x16, other arithmetic, turn(): return jax.tree.map(lambda a, b: jnp.where(reached, a, b), new, before)  83.3 us
    all_gather x1, waiting for transfers between devices, on_device(): lax.all_gather(w_bc, 'ctx', axis=0, tiled=True)  77.4 us
    dot_general x4, matrix products, make_folder(): jnp.dot(source, piece.reshape(piece_rows, -1), preferred_element_type=jnp...  73.1 us
    dynamic_slice x32, local copies, waits for them, and re-layouts, turn(): part[k].astype(own.dtype)  38.4 us
    reshape x2, local copies, waits for them, and re-layouts, on_device(): scan_out.reshape(tok_rows, inner_width)  31.1 us
  transfers between devices with their start and end apart: 6, of which 6 were waited for; matrix products, arithmetic and copies ran while one was open for 21% of the time, Pallas kernels for 0%

commit v1 on v0

v1 whole, which is shorter than its diff:
```python
import jax
import jax.numpy as jnp
from jax import lax
from jax.sharding import PartitionSpec as P

SPAN = 256
F32 = jnp.float32
BF16 = jnp.bfloat16


def exchange_columns(value, groups, count):
    if count == 1:
        return value
    rows = value.shape[0]
    parts = value.reshape(rows, count, -1)
    got = lax.all_to_all(
        parts.swapaxes(0, 1), "ctx", 0, 0, axis_index_groups=groups, tiled=True
    )
    return got.reshape(count * rows, -1)


def on_device(
    tokens,
    w_z,
    w_x,
    w_bc,
    w_dt,
    conv_x,
    conv_bc,
    bias_x,
    bias_bc,
    dt_bias,
    a_log,
    d_skip,
    norm_gain,
):
    own_rows = tokens.shape[0]
    kernel = conv_x.shape[0]
    group_count = w_bc.shape[1]
    bc_width = w_bc.shape[2]
    state_size = bc_width // 2
    heads = w_dt.shape[1] // group_count
    width = w_x.shape[1] // group_count
    head_dim = width // heads
    devices = lax.axis_size("ctx")
    plane = group_count
    depth = devices // plane
    mine = lax.axis_index("ctx")
    column, level = mine % plane, mine // plane
    in_plane = [[z * plane + i for i in range(plane)] for z in range(depth)]
    along = [[z * plane + i for z in range(depth)] for i in range(plane)]

    def take(value):
        size = value.shape[-1] // plane
        return lax.dynamic_slice_in_dim(value, column * size, size, axis=value.ndim - 1)

    k_rows = w_x.shape[0]
    main = jnp.concatenate(
        [
            w_x.reshape(k_rows, plane, width),
            w_bc,
            w_dt.reshape(k_rows, plane, heads),
        ],
        axis=2,
    ).reshape(k_rows, -1)
    main = exchange_columns(main, in_plane, plane)
    main = lax.all_gather(main, "ctx", axis=0, tiled=True, axis_index_groups=along)
    if plane > 1:
        toks = lax.all_gather(tokens, "ctx", axis=0, tiled=True, axis_index_groups=in_plane)
    else:
        toks = tokens
    w_gate = exchange_columns(w_z, in_plane, plane)
    w_gate = lax.all_gather(w_gate, "ctx", axis=0, tiled=True, axis_index_groups=along)
    rows = toks.shape[0]
    blocks = rows // SPAN

    projected = jnp.dot(toks, main, preferred_element_type=F32)
    step_sum = projected[:, width + bc_width :]
    mixed = projected[:, : width + bc_width].astype(BF16)
    edge = lax.ppermute(
        mixed[rows - (kernel - 1) :],
        "ctx",
        [(i, i + plane) for i in range(devices - plane)],
    )
    extended = jnp.concatenate([edge, mixed], axis=0)
    taps = jnp.concatenate([take(conv_x), take(conv_bc.reshape(kernel, -1))], axis=1)
    offset = jnp.concatenate([take(bias_x), take(bias_bc.reshape(-1))])
    running = jnp.zeros((rows, width + bc_width), F32) + offset[None, :]
    for tap in range(kernel):
        running = running + taps[tap][None, :] * extended[tap : tap + rows].astype(F32)
    conv = jax.nn.silu(running).astype(BF16)
    inner = conv[:, :width].reshape(blocks, SPAN, heads, head_dim)
    b_in = conv[:, width : width + state_size].reshape(blocks, SPAN, state_size)
    c_in = conv[:, width + state_size :].reshape(blocks, SPAN, state_size)

    step = jax.nn.softplus(step_sum + take(dt_bias)[None, :])
    log_rate = -jnp.exp(take(a_log))[None, :] * step
    cumul = jnp.cumsum(log_rate.reshape(blocks, SPAN, heads), axis=1)
    step = step.reshape(blocks, SPAN, heads)
    scores = jnp.einsum("cin,cjn->cij", c_in, b_in, preferred_element_type=F32)
    cumul_t = jnp.swapaxes(cumul, 1, 2)
    step_t = jnp.swapaxes(step, 1, 2)
    gap = cumul_t[:, :, :, None] - cumul_t[:, :, None, :]
    causal = jnp.arange(SPAN)[:, None] >= jnp.arange(SPAN)[None, :]
    decay = jnp.where(causal[None, None], jnp.exp(jnp.minimum(gap, 0.0)), 0.0)
    weight = (scores[:, None] * decay * step_t[:, :, None, :]).astype(BF16)
    intra = jnp.einsum("chij,cjhp->cihp", weight, inner, preferred_element_type=F32)
    block_log = cumul[:, -1, :]
    weighted_b = (
        (jnp.exp(block_log[:, None, :] - cumul) * step)[..., None]
        * b_in[:, :, None, :].astype(F32)
    ).astype(BF16)
    local = jnp.einsum("cjhn,cjhp->chnp", weighted_b, inner, preferred_element_type=F32)
    state = jnp.zeros((heads, state_size, head_dim), F32)
    before = jnp.zeros((heads,), F32)
    starts, befores = [], []
    for block in range(blocks):
        starts.append(state)
        befores.append(before)
        state = jnp.exp(block_log[block])[:, None, None] * state + local[block]
        before = before + block_log[block]
    starts = jnp.stack(starts).astype(BF16)
    inter = jnp.einsum("cin,chnp->cihp", c_in, starts, preferred_element_type=F32)
    scan = (
        intra
        + inter * jnp.exp(cumul)[..., None]
        + take(d_skip)[None, None, :, None] * inner.astype(F32)
    ).reshape(rows, width)
    reach = jnp.exp(cumul + jnp.stack(befores)[:, None, :]).reshape(rows, heads)

    high = lax.reduce_precision(before, 8, 7)
    low = before - high
    logs = jnp.stack([high, low]).astype(BF16)
    packed = jnp.concatenate(
        [
            state.transpose(1, 0, 2).reshape(state_size, width).astype(BF16),
            jnp.repeat(logs, head_dim, axis=1),
        ]
    )
    everyone = lax.all_gather(packed, "ctx", axis_index_groups=along)
    all_logs = (
        everyone[:, state_size].astype(F32) + everyone[:, state_size + 1].astype(F32)
    )
    order = jnp.arange(depth)
    between = (order[None, :] > order[:, None]) & (order[None, :] < level)
    factor = jnp.exp(jnp.sum(jnp.where(between[:, :, None], all_logs[None], 0.0), axis=1))
    factor = jnp.where((order < level)[:, None], factor, 0.0)
    carried = jnp.sum(everyone[:, :state_size].astype(F32) * factor[:, None, :], axis=0)
    far = jnp.dot(
        c_in.reshape(rows, state_size), carried.astype(BF16), preferred_element_type=F32
    )
    scan = (
        scan.reshape(rows, heads, head_dim)
        + far.reshape(rows, heads, head_dim) * reach[:, :, None]
    ).reshape(rows, width)

    gate = jnp.dot(toks, w_gate, preferred_element_type=F32).astype(BF16).astype(F32)
    gated = scan * jax.nn.silu(gate)
    scale = lax.rsqrt(jnp.mean(gated * gated, axis=-1, keepdims=True) + 1e-05)
    result = (gated * scale * take(norm_gain)[None, :]).astype(BF16)
    if plane == 1:
        return result
    back = lax.all_to_all(
        result.reshape(plane, own_rows, width), "ctx", 0, 0, axis_index_groups=in_plane, tiled=True
    )
    return back.swapaxes(0, 1).reshape(own_rows, plane * width)


def solution(mesh):
    placed = (
        P("ctx", None),
        P("ctx", "grp"),
        P("ctx", "grp"),
        P("ctx", "grp", None),
        P("ctx", "grp"),
        P(None, "grp"),
        P(None, "grp", None),
        P("grp"),
        P("grp", None),
        P("grp"),
        P("grp"),
        P("grp"),
        P("grp"),
    )
    return jax.shard_map(
        on_device, mesh=mesh, in_specs=placed, out_specs=P("ctx", "grp"), check_vma=False
    )
```

time: 1190 us -> 757 us (0.64)
  waiting for transfers between devices: 711 us -> 425 us
  other arithmetic: 115 us -> 33 us
  local copies, waits for them, and re-layouts: 155 us -> 77.1 us
  blocking collectives: 56.6 us -> 110 us
  matrix products: 117 us -> 92.5 us
    all_gather x4, waiting for transfers between devices: 707 us -> 424 us  [the longest x1 160 us: on_device(): lax.all_gather(tokens, 'ctx', axis=0, tiled=True, axis_index_groups=in_pl...]
    all_to_all x0 -> x3, blocking collectives: none -> 110 us  [the longest x2 60.5 us: exchange_columns(): lax.all_to_all(parts.swapaxes(0, 1), 'ctx', 0, 0, axis_index_groups=group...]
    select_n x16 -> x1, other arithmetic: 83.3 us -> 0.07 us  [on_device(): factor = jnp.where((order < level)[:, None], factor, 0.0)]
    all_gather x2 -> x0, blocking collectives: 56.6 us -> none  [the longest x1 30.9 us: on_device(): lax.all_gather(w_dt, 'ctx', axis=0, tiled=True)]
    reshape x7 -> x5, local copies, waits for them, and re-layouts: 55.1 us -> 4.7 us  [the longest x1 2.45 us: on_device(): return back.swapaxes(0, 1).reshape(own_rows, plane * width)]
    dynamic_slice x32 -> x8, local copies, waits for them, and re-layouts: 38.4 us -> 1.44 us  [take(): lax.dynamic_slice_in_dim(value, column * size, size, axis=value.ndim - 1)]
    dot_general x8 -> x6, matrix products: 117 us -> 88 us  [the longest x1 28.8 us: on_device(): projected = jnp.dot(toks, main, preferred_element_type=F32)]
    another operation x1 -> x6, local copies, waits for them, and re-layouts: 0.01 us -> 29.1 us  [the longest x2 29 us: on_device(): scan.reshape(rows, heads, head_dim)]
  transfers between devices with their start and end apart: 6 -> 5, of which waited for: 6 -> 3; matrix products, arithmetic and copies ran while one was open for 21% -> 18% of each run, Pallas kernels for 0% -> 0%
where the time goes in v1:
time: 757 us; the launch traced here: 753 us
  waiting for transfers between devices  425 us (56%)
  blocking collectives  110 us (15%)
  matrix products  92.5 us (12%)
  local copies, waits for them, and re-layouts  77.1 us (10%)
  other arithmetic  33 us (4%)
  between operations  13.7 us (2%)
    all_gather x1, waiting for transfers between devices, on_device(): lax.all_gather(tokens, 'ctx', axis=0, tiled=True, axis_index_groups=in_pl...  160 us
    all_gather x1, waiting for transfers between devices, on_device(): lax.all_gather(main, 'ctx', axis=0, tiled=True, axis_index_groups=along)  149 us
    all_gather x1, waiting for transfers between devices, on_device(): lax.all_gather(w_gate, 'ctx', axis=0, tiled=True, axis_index_groups=along)  116 us
    all_to_all x2, blocking collectives, exchange_columns(): lax.all_to_all(parts.swapaxes(0, 1), 'ctx', 0, 0, axis_index_groups=group...  60.5 us
    all_to_all x1, blocking collectives, on_device(): lax.all_to_all(result.reshape(plane, own_rows, width), 'ctx', 0, 0, axis_...  49.6 us
    another operation x2, local copies, waits for them, and re-layouts, on_device(): scan.reshape(rows, heads, head_dim)  29 us
    dot_general x1, matrix products, on_device(): projected = jnp.dot(toks, main, preferred_element_type=F32)  28.8 us
    dot_general x1, matrix products, on_device(): jnp.dot(toks, w_gate, preferred_element_type=F32).astype(BF16).astype(F32)  23.6 us
  transfers between devices with their start and end apart: 5, of which 3 were waited for; matrix products, arithmetic and copies ran while one was open for 18% of the time, Pallas kernels for 0%

profile of v1, /device:TPU:27, one launch (start us, length us, event | category | flops | bytes accessed | tf_op | source)
XLA Modules:
  0.0 753.1 jit_solution(2936748826411546368)
XLA Ops:
  6.5 1.4 copy.100
  7.9 3.3 copy.99
  12.1 33.0 %all_to_all.15 = bf16[4,256,1296]{1,2,0:T(8,128)(2,1)S(1)} all-to-all(bf16[4,256,1296]{1,2,0:T(8,128)(2,1)S(1)} %maximum_bitcast_fusion), channel_id=1, replica_groups={{0,2,4,6},{8,10,12,14},{16,18,20,22},{24,26,28,30},{1,3,5,7},{9,11,13,1..., dimensions={0} | all-to-all | bytes 5308416 | tf_op jit(solution)/shard_map/all_to_all | solution.py:16
  45.1 1.9 copy.132
  47.9 2.5 copy.121
  50.4 27.5 %all_to_all.16 = bf16[4,256,1024]{1,2,0:T(8,128)(2,1)S(1)} all-to-all(bf16[4,256,1024]{1,2,0:T(8,128)(2,1)} %bitcast.189), channel_id=1, replica_groups={{0,2,4,6},{8,10,12,14},{16,18,20,22},{24,26,28,30},{1,3,5,7},{9,11,13,1..., dimensions={0} | all-to-all | bytes 4194304 | tf_op jit(solution)/shard_map/all_to_all | solution.py:16
  77.8 2.4 copy.122
  83.4 148.6 %all-gather.7.cloned.1.call-done = bf16[4096,1296]{0,1:T(8,128)(2,1)} async-done(((bf16[1024,1296]{0,1:T(8,128)(2,1)}), bf16[4096,1296]{0,1:T(8,128)(2,1)}) %all-gather.7.cloned.1.call-update) | async-done | bytes 10616848 | tf_op jit(solution)/shard_map/all_gather | solution.py:67
  232.1 160.1 %all-gather.9.cloned.1.call-done = bf16[2048,4096]{1,0:T(8,128)(2,1)} async-done(((bf16[512,4096]{1,0:T(8,128)(2,1)}), bf16[2048,4096]{1,0:T(8,128)(2,1)}) %all-gather.9.cloned.1.call-update) | async-done | bytes 16777232 | tf_op jit(solution)/shard_map/all_gather | solution.py:69
  392.1 28.8 %fusion.51 = (bf16[2048,1296]{0,1:T(8,128)(2,1)S(1)}, f32[2048,1296]{0,1:T(8,128)S(1)}) fusion(bf16[4096,1296]{0,1:T(8,128)(2,1)} %all-gather.7.cloned.1.call-done, bf16[2048,4096]{1,0:T(8,128)(2,1)} %all-gather.9.cloned.1.call-done), kind=kOutput, calls=%fused_computation.145 | convolution fusion | flops 21745926144 | bytes 43319296 | tf_op jit(solution)/shard_map/dot_general | solution.py:77
  421.0 2.3 copy-done.3
  423.4 1.5 collective-permute-start
  425.1 4.6 reduce-window.6
  432.1 115.6 %all-gather.11.cloned.1.call-done = bf16[4096,1024]{1,0:T(8,128)(2,1)} async-done(((bf16[1024,1024]{1,0:T(8,128)(2,1)}), bf16[4096,1024]{1,0:T(8,128)(2,1)}) %all-gather.11.cloned.1.call-update) | async-done | bytes 8388624 | tf_op jit(solution)/shard_map/all_gather | solution.py:73
  547.7 23.6 %fusion.53 = bf16[2048,1024]{1,0:T(8,128)(2,1)} fusion(bf16[2048,4096]{1,0:T(8,128)(2,1)} %all-gather.9.cloned.1.call-done, bf16[4096,1024]{1,0:T(8,128)(2,1)} %all-gather.11.cloned.1.call-done), kind=kOutput, calls=%fused_computation.147 | convolution fusion | flops 17179869184 | bytes 29360128 | tf_op jit(solution)/shard_map/dot_general | solution.py:157
  571.3 5.7 slice.169
  577.2 4.3 mul.339
  581.5 9.3 %copy.119 = f32[2048,1024]{1,0:T(8,128)} copy(f32[2048,1024]{0,1:T(8,128)} %bitcast.181) | data formatting | bytes 16777216 | tf_op jit(solution)/shard_map/mul | solution.py:154
  590.9 18.7 %multiply_convert_fusion.3 = bf16[2048,1280]{0,1:T(8,128)(2,1)S(1)} fusion(bf16[2048,1280]{0,1:T(8,128)(2,1)} %slice.169, bf16[3,1280]{0,1:T(8,128)(2,1)S(1)} %collective-permute-done, f32[1280]{0:T(1024)S(1)} %get-tuple-element.23, f32[1280]{0:T(1024)S(1)} %get-tuple-element.24, f32[1280]{0:T(1024)S(1)} %get-tuple-element.22, ...), kind=kLoop, calls=%fused_computation.11 | loop fusion | flops 68157440 | bytes 10519040 | tf_op jit(solution)/shard_map/convert_element_type | solution.py:91
  609.7 2.3 copy-done.2
  612.0 2.3 slice.178
  615.2 3.8 copy.138
  619.1 7.6 %fusion.11 = f32[8,16,128,64]{2,3,1,0:T(8,128)S(1)} fusion(f32[8,256,128]{2,1,0:T(8,128)S(1)} %copy.112, f32[8,256,16]{1,2,0:T(8,128)} %get-tuple-element.44, bf16[8,256,16,64]{1,0,3,2:T(8,128)(2,1)S(1)} %bitcast.195), kind=kOutput, calls=%fused_computation.17 | convolution fusion | flops 545259520 | bytes 9568256 | tf_op jit(solution)/shard_map/cjhn,cjhp->chnp/dot_general | solution.py:113
  628.1 4.5 fusion.52
  634.3 18.4 %fusion.12 = f32[8,256,16,64]{1,3,2,0:T(8,128)} fusion(f32[8,256,16,64]{1,3,2,0:T(8,128)} %bitcast.187, f32[16]{0:T(128)S(1)} %copy-done.17, f32[8,256,16]{1,2,0:T(8,128)} %get-tuple-element.43, f32[8,16,256]{2,1,0:T(8,128)S(1)} %copy.109, f32[8,16,256]{2,1,0:T(8,128)S(1)} %get-tuple-element.45, f32[8,256,256]{2,1,0:T(8,128)S(1)} %fusion.19, ...), kind=kOutput, calls=%fused_computation.19 | convolution fusion | flops 1134559232 | bytes 23527488 | tf_op jit(solution)/shard_map/chij,cjhp->cihp/dot_general | solution.py:107
  652.7 14.6 %copy.124 = f32[8,256,16,64]{3,2,1,0:T(8,128)} copy(f32[8,256,16,64]{1,3,2,0:T(8,128)} %fusion.12) | data formatting | bytes 16777216 | tf_op jit(solution)/shard_map/reshape;reshape | solution.py:153
  667.3 14.5 %reshape.496 = f32[2048,1024]{1,0:T(8,128)} reshape(f32[8,256,16,64]{3,2,1,0:T(8,128)} %copy.124) | data formatting | bytes 16777216 | tf_op jit(solution)/shard_map/reshape;reshape | solution.py:153
  681.8 0.9 fusion.35
  682.9 1.4 multiply_reduce_fusion.1
  684.4 9.1 %multiply_reduce_fusion = (f32[2048]{0:T(1024)S(1)}, f32[2048,1024]{1,0:T(8,128)S(1)}) fusion(bf16[2048,1024]{1,0:T(8,128)(2,1)} %fusion.53, f32[2048,1024]{1,0:T(8,128)} %reshape.496, f32[2048,1024]{1,0:T(8,128)} %copy.119, bf16[128,1024]{1,0:T(8,128)(2,1)S(1)} %multiply_reduce_fusion.1, bf16[2048,1280]{0,1:T(8,128)(2,1)} %copy-done.2), kind=kOutput, calls=%fused_computation.21 | convolution fusion | flops 557840384 | bytes 30154752 | tf_op jit(solution)/shard_map/dot_general | solution.py:149
  694.4 49.6 %all_to_all.17 = bf16[4,512,1024]{2,1,0:T(8,128)(2,1)S(1)} all-to-all(bf16[4,512,1024]{2,1,0:T(8,128)(2,1)S(1)} %bitcast.182), channel_id=1, replica_groups={{0,2,4,6},{8,10,12,14},{16,18,20,22},{24,26,28,30},{1,3,5,7},{9,11,13,1..., dimensions={0} | all-to-all | bytes 8388608 | tf_op jit(solution)/shard_map/all_to_all | solution.py:163
  744.1 2.5 copy.135
  (105 shorter events, 12.9 us)
Async XLA Ops:
  6.5 75.3 %copy-start = (f32[4,4096]{1,0:T(4,128)S(1)}, f32[4,4096]{1,0:T(4,128)}, u32[]{:S(2)}) copy-start(f32[4,4096]{1,0:T(4,128)} %param.18) | copy-start | bytes 196612
  6.5 225.5 %all-gather.7.cloned.1.call-start = ((), (), s32[]{:S(2)}) async-start(), calls=%async_computation.3 | async-start | bytes 13271040 | tf_op jit(solution)/shard_map/all_gather | solution.py:67
  12.1 35.8 %copy-start.6 = (bf16[256,4096]{1,0:T(8,128)(2,1)S(1)}, bf16[256,4096]{1,0:T(8,128)(2,1)}, u32[]{:S(2)}) copy-start(bf16[256,4096]{1,0:T(8,128)(2,1)} %param.14) | copy-start | bytes 6291460
  47.0 345.1 %all-gather.9.cloned.1.call-start = ((), (), s32[]{:S(2)}) async-start(), calls=%async_computation.4 | async-start | bytes 20971520 | tf_op jit(solution)/shard_map/all_gather | solution.py:69
  47.8 32.6 %copy-start.7 = (f32[4,4,256]{2,1,0:T(4,128)S(1)}, f32[4,4,256]{2,1,0:T(4,128)}, u32[]{:S(2)}) copy-start(f32[4,4,256]{2,1,0:T(4,128)} %param.19) | copy-start | bytes 49156
  47.8 32.6 %copy-start.9 = (f32[4,256]{1,0:T(4,128)S(1)}, f32[4,256]{1,0:T(4,128)}, u32[]{:S(2)}) copy-start(f32[4,256]{1,0:T(4,128)} %param.21) | copy-start | bytes 12292
  47.8 32.6 %copy-start.14 = (f32[64]{0:T(128)S(1)}, f32[64]{0:T(128)}, u32[]{:S(2)}) copy-start(f32[64]{0:T(128)} %param.22) | copy-start | bytes 772
  47.8 32.7 %copy-start.15 = (f32[64]{0:T(128)S(1)}, f32[64]{0:T(128)}, u32[]{:S(2)}) copy-start(f32[64]{0:T(128)} %param.24) | copy-start | bytes 772
  47.8 34.1 %copy-start.16 = (f32[64]{0:T(128)S(1)}, f32[64]{0:T(128)}, u32[]{:S(2)}) copy-start(f32[64]{0:T(128)} %param.23) | copy-start | bytes 772
  47.8 499.9 %all-gather.11.cloned.1.call-start = ((), (), s32[]{:S(2)}) async-start(), calls=%async_computation.5 | async-start | bytes 10485760 | tf_op jit(solution)/shard_map/all_gather | solution.py:73
  80.3 601.5 %all-gather.13.cloned.1.call-start = ((), (), s32[]{:S(2)}) async-start(), calls=%async_computation.6 | async-start | bytes 1392640 | tf_op jit(solution)/shard_map/all_gather | solution.py:140
  82.0 150.0 %copy-start.11 = (pred[4]{0:T(512)(128)(4,1)}, pred[4]{0:T(512)(128)(4,1)S(1)}, u32[]{:S(2)}) copy-start(pred[4]{0:T(512)(128)(4,1)S(1)} %iota_compare_fusion.2) | copy-start | bytes 16
  421.0 2.3 copy-start.3
  423.4 167.4 %collective-permute-start = (bf16[3,1280]{0,1:T(8,128)(2,1)S(1)}, bf16[3,1280]{0,1:T(8,128)(2,1)S(1)}, u32[]{:S(2)}, u32[]{:S(2)}) collective-permute-start(bf16[3,1280]{0,1:T(8,128)(2,1)S(1)} %slice.168), channel_id=1, source_target_pairs={{0,8},{2,10},{4,12},{6,14},{8,16},{10,18},{12,20},{14,22},{16,24},... | collective-permute-start | bytes 23048 | tf_op jit(solution)/shard_map/ppermute | solution.py:80
  609.6 2.4 copy-start.2
  615.2 11.5 %copy-start.5 = (bf16[8,16,128,64]{2,3,1,0:T(8,128)(2,1)S(1)}, bf16[8,16,128,64]{2,3,1,0:T(8,128)(2,1)}, u32[]{:S(2)}) copy-start(bf16[8,16,128,64]{2,3,1,0:T(8,128)(2,1)} %broadcast_dynamic-update-slice_fusion) | copy-start | bytes 6291460
  619.0 8.5 %copy-start.4 = (bf16[128,8,8,256]{3,2,1,0:T(8,128)(2,1)}, bf16[128,8,8,256]{3,2,1,0:T(8,128)(2,1)S(1)}, u32[]{:S(2)}) copy-start(bf16[128,8,8,256]{3,2,1,0:T(8,128)(2,1)S(1)} %copy.138) | copy-start | bytes 12582916
  619.0 8.2 %copy-start.8 = (f32[16]{0:T(128)S(1)}, f32[16]{0:T(128)}, u32[]{:S(2)}) copy-start(f32[16]{0:T(128)} %get-tuple-element.16) | copy-start | bytes 196
  627.7 5.3 copy-start.10
  628.1 6.3 copy-start.17
  667.3 15.4 %copy-start.13 = (pred[4,4]{1,0:T(4,128)(4,1)S(1)}, pred[4,4]{1,0:T(4,128)(4,1)}, u32[]{:S(2)}) copy-start(pred[4,4]{1,0:T(4,128)(4,1)} %fusion.45) | copy-start | bytes 52
  667.3 15.6 %copy-start.12 = (pred[4]{0:T(512)(128)(4,1)S(1)}, pred[4]{0:T(512)(128)(4,1)}, u32[]{:S(2)}) copy-start(pred[4]{0:T(512)(128)(4,1)} %copy-done.11) | copy-start | bytes 16
  684.4 9.1 %dynamic-slice-start = ((f32[4096]{0:T(1024)}, s32[]{:T(128)}), f32[1024]{0:T(1024)S(1)}, s32[]{:S(2)}) async-start(f32[4096]{0:T(1024)} %param.25, s32[]{:T(128)} %select_n.46), calls=%async_computation.7 | async-start | bytes 8704 | tf_op jit(solution)/shard_map/dynamic_slice | solution.py:55
  694.4 52.1 %copy-start.1 = (f32[4,4096]{1,0:T(4,128)S(1)}, f32[4,4096]{1,0:T(4,128)}, u32[]{:S(2)}) copy-start(f32[4,4096]{1,0:T(4,128)} %param.18) | copy-start | bytes 196612
Sparse Core Ops, SparseCore 0:
  47.1 184.8 all-gather.6
  233.9 158.2 all-gather.8
  393.7 153.9 all-gather.10
  634.4 28.4 all-gather.12

commit v2 on v1

--- a/solution.py
+++ b/solution.py
@@ -17,6 +17,26 @@
         parts.swapaxes(0, 1), "ctx", 0, 0, axis_index_groups=groups, tiled=True
     )
     return got.reshape(count * rows, -1)
+
+
+def swapped(value, step, plane):
+    pairs = [(i, i - i % plane + (i % plane ^ step)) for i in range(lax.axis_size("ctx"))]
+    return lax.ppermute(value, "ctx", pairs)
+
+
+def earlier_parts(value, along, plane, depth):
+    if depth <= 4:
+        for back in range(1, depth):
+            pairs = [(i, i + back * plane) for i in range((depth - back) * plane)]
+            yield lax.ppermute(value, "ctx", pairs)
+    else:
+        everyone = lax.all_gather(value, "ctx", axis_index_groups=along)
+        level = lax.axis_index("ctx") // plane
+        for back in range(1, depth):
+            part = lax.dynamic_index_in_dim(
+                everyone, jnp.maximum(level - back, 0), keepdims=False
+            )
+            yield jnp.where(back <= level, part, 0)
 
 
 def on_device(
@@ -46,7 +66,7 @@
     plane = group_count
     depth = devices // plane
     mine = lax.axis_index("ctx")
-    column, level = mine % plane, mine // plane
+    column = mine % plane
     in_plane = [[z * plane + i for i in range(plane)] for z in range(depth)]
     along = [[z * plane + i for z in range(depth)] for i in range(plane)]
 
@@ -64,19 +84,23 @@
         axis=2,
     ).reshape(k_rows, -1)
     main = exchange_columns(main, in_plane, plane)
+    main, tokens, w_z = lax.optimization_barrier((main, tokens, w_z))
     main = lax.all_gather(main, "ctx", axis=0, tiled=True, axis_index_groups=along)
-    if plane > 1:
-        toks = lax.all_gather(tokens, "ctx", axis=0, tiled=True, axis_index_groups=in_plane)
-    else:
-        toks = tokens
+    pieces = [tokens] + [swapped(tokens, step, plane) for step in range(1, plane)]
     w_gate = exchange_columns(w_z, in_plane, plane)
     w_gate = lax.all_gather(w_gate, "ctx", axis=0, tiled=True, axis_index_groups=along)
-    rows = toks.shape[0]
+    rows = own_rows * plane
     blocks = rows // SPAN
 
-    projected = jnp.dot(toks, main, preferred_element_type=F32)
-    step_sum = projected[:, width + bc_width :]
-    mixed = projected[:, : width + bc_width].astype(BF16)
+    mixed = jnp.zeros((rows, width + bc_width), BF16)
+    step_sum = jnp.zeros((rows, heads), F32)
+    for step, piece in enumerate(pieces):
+        projected = jnp.dot(piece, main, preferred_element_type=F32)
+        at = ((column ^ step) * own_rows, 0)
+        mixed = lax.dynamic_update_slice(
+            mixed, projected[:, : width + bc_width].astype(BF16), at
+        )
+        step_sum = lax.dynamic_update_slice(step_sum, projected[:, width + bc_width :], at)
     edge = lax.ppermute(
         mixed[rows - (kernel - 1) :],
         "ctx",
@@ -137,15 +161,12 @@
             jnp.repeat(logs, head_dim, axis=1),
         ]
     )
-    everyone = lax.all_gather(packed, "ctx", axis_index_groups=along)
-    all_logs = (
-        everyone[:, state_size].astype(F32) + everyone[:, state_size + 1].astype(F32)
-    )
-    order = jnp.arange(depth)
-    between = (order[None, :] > order[:, None]) & (order[None, :] < level)
-    factor = jnp.exp(jnp.sum(jnp.where(between[:, :, None], all_logs[None], 0.0), axis=1))
-    factor = jnp.where((order < level)[:, None], factor, 0.0)
-    carried = jnp.sum(everyone[:, :state_size].astype(F32) * factor[:, None, :], axis=0)
+    carried = jnp.zeros((state_size, width), F32)
+    skipped = jnp.zeros((width,), F32)
+    for part in earlier_parts(packed, along, plane, depth):
+        part = part.astype(F32)
+        carried = carried + jnp.exp(skipped)[None, :] * part[:state_size]
+        skipped = skipped + part[state_size] + part[state_size + 1]
     far = jnp.dot(
         c_in.reshape(rows, state_size), carried.astype(BF16), preferred_element_type=F32
     )
@@ -154,16 +175,19 @@
         + far.reshape(rows, heads, head_dim) * reach[:, :, None]
     ).reshape(rows, width)
 
-    gate = jnp.dot(toks, w_gate, preferred_element_type=F32).astype(BF16).astype(F32)
-    gated = scan * jax.nn.silu(gate)
-    scale = lax.rsqrt(jnp.mean(gated * gated, axis=-1, keepdims=True) + 1e-05)
-    result = (gated * scale * take(norm_gain)[None, :]).astype(BF16)
-    if plane == 1:
-        return result
-    back = lax.all_to_all(
-        result.reshape(plane, own_rows, width), "ctx", 0, 0, axis_index_groups=in_plane, tiled=True
-    )
-    return back.swapaxes(0, 1).reshape(own_rows, plane * width)
+    scan, w_gate = lax.optimization_barrier((scan, w_gate))
+    gain = take(norm_gain)[None, :]
+    out = jnp.zeros((own_rows, plane * width), BF16)
+    for step in reversed(range(plane)):
+        gate = jnp.dot(pieces[step], w_gate, preferred_element_type=F32).astype(BF16)
+        part = lax.dynamic_slice_in_dim(scan, (column ^ step) * own_rows, own_rows)
+        gated = part * jax.nn.silu(gate.astype(F32))
+        scale = lax.rsqrt(jnp.mean(gated * gated, axis=-1, keepdims=True) + 1e-05)
+        result = (gated * scale * gain).astype(BF16)
+        if step:
+            result = swapped(result, step, plane)
+        out = lax.dynamic_update_slice(out, result, (0, (column ^ step) * width))
+    return out
 
 
 def solution(mesh):

time: 757 us -> 542 us (0.72)
  the two profiles are of different devices: /device:TPU:27 before, /device:TPU:0 now
where the time goes in v2:
time: 542 us; the launch traced here: 531 us
  waiting for transfers between devices  209 us (39%)
  local copies, waits for them, and re-layouts  115 us (21%)
  matrix products  101 us (19%)
  blocking collectives  36.6 us (7%)
  other arithmetic  30.5 us (6%)
  starting transfers between devices  24.2 us (4%)
  between operations  14.5 us (3%)
    all_to_all x1, waiting for transfers between devices, exchange_columns(): lax.all_to_all(parts.swapaxes(0, 1), 'ctx', 0, 0, axis_index_groups=group...  102 us
    all_gather x1, waiting for transfers between devices, on_device(): lax.all_gather(main, 'ctx', axis=0, tiled=True, axis_index_groups=along)  66.8 us
    ppermute x6, waiting for transfers between devices, swapped(): return lax.ppermute(value, 'ctx', pairs)  40.2 us
    dot_general x4, matrix products, on_device(): projected = jnp.dot(piece, main, preferred_element_type=F32)  38.9 us
    all_to_all x1, blocking collectives, exchange_columns(): lax.all_to_all(parts.swapaxes(0, 1), 'ctx', 0, 0, axis_index_groups=group...  36.6 us
    another operation x2, local copies, waits for them, and re-layouts, on_device(): scan.reshape(rows, heads, head_dim)  29 us
    dot_general x4, matrix products, on_device(): jnp.dot(pieces[step], w_gate, preferred_element_type=F32).astype(BF16)  28.9 us
    reshape x2, local copies, waits for them, and re-layouts, on_device(): inner = conv[:, :width].reshape(blocks, SPAN, heads, head_dim)  21.9 us
  transfers between devices with their start and end apart: 13, of which 5 were waited for; matrix products, arithmetic and copies ran while one was open for 38% of the time, Pallas kernels for 0%

profile of v2, /device:TPU:0, one launch (start us, length us, event | category | flops | bytes accessed | tf_op | source)
XLA Modules:
  0.0 531.5 jit_solution(7183539448715090415)
XLA Ops:
  6.5 3.3 copy.81
  10.4 36.6 %all_to_all.10 = bf16[4,256,1296]{1,2,0:T(8,128)(2,1)S(1)} all-to-all(bf16[4,256,1296]{1,2,0:T(8,128)(2,1)S(1)} %maximum_bitcast_fusion), channel_id=1, replica_groups={{0,2,4,6},{8,10,12,14},{16,18,20,22},{24,26,28,30},{1,3,5,7},{9,11,13,1..., dimensions={0} | all-to-all | bytes 5308416 | tf_op jit(solution)/shard_map/all_to_all | solution.py:16
  52.1 3.7 all-to-all-start.1
  63.1 102.2 %all-to-all-done.1 = bf16[4,256,1024]{1,2,0:T(8,128)(2,1)S(1)} async-done(((bf16[4,256,1024]{1,2,0:T(8,128)(2,1)}), bf16[4,256,1024]{1,2,0:T(8,128)(2,1)S(1)}, u32[]{:S(2)}, u32[]{:S(2)}) %all-to-all-start.1) | async-done | bytes 2097184 | tf_op jit(solution)/shard_map/all_to_all | solution.py:16
  167.7 66.8 %all-gather.3.cloned.1.call-done = bf16[4096,1296]{0,1:T(8,128)(2,1)} async-done(((bf16[1024,1296]{0,1:T(8,128)(2,1)}), bf16[4096,1296]{0,1:T(8,128)(2,1)}) %all-gather.3.cloned.1.call-update) | async-done | bytes 10616848 | tf_op jit(solution)/shard_map/all_gather | solution.py:88
  234.6 9.8 %fusion.65 = f32[512,1296]{0,1:T(8,128)S(1)} fusion(bf16[512,4096]{1,0:T(8,128)(2,1)} %param.13, bf16[4096,1296]{0,1:T(8,128)(2,1)} %all-gather.3.cloned.1.call-done), kind=kOutput, calls=%fused_computation.186 | convolution fusion | flops 5435817984 | bytes 17465344 | tf_op jit(solution)/shard_map/dot_general | solution.py:98
  244.5 10.1 %fusion.66 = f32[512,1296]{0,1:T(8,128)S(1)} fusion(bf16[512,4096]{1,0:T(8,128)(2,1)} %collective-permute-done, bf16[4096,1296]{0,1:T(8,128)(2,1)S(1)} %copy-done.33), kind=kOutput, calls=%fused_computation.187 | convolution fusion | flops 5435817984 | bytes 17465344 | tf_op jit(solution)/shard_map/dot_general | solution.py:98
  254.6 4.4 collective-permute-done.1
  259.0 9.1 %fusion.67 = f32[512,1296]{0,1:T(8,128)S(1)} fusion(bf16[512,4096]{1,0:T(8,128)(2,1)} %collective-permute-done.1, bf16[4096,1296]{0,1:T(8,128)(2,1)S(1)} %copy-done.33), kind=kOutput, calls=%fused_computation.188 | convolution fusion | flops 5435817984 | bytes 17465344 | tf_op jit(solution)/shard_map/dot_general | solution.py:98
  268.1 10.0 %fusion.68 = f32[512,1296]{0,1:T(8,128)S(1)} fusion(bf16[512,4096]{1,0:T(8,128)(2,1)} %collective-permute-done.2, bf16[4096,1296]{0,1:T(8,128)(2,1)S(1)} %copy-done.33), kind=kOutput, calls=%fused_computation.189 | convolution fusion | flops 5435817984 | bytes 17465344 | tf_op jit(solution)/shard_map/dot_general | solution.py:98
  279.6 4.6 reduce-window.6
  290.3 3.0 slice.397
  293.3 3.0 slice.396
  306.9 3.6 collective-permute-start.3
  312.2 4.3 mul.454
  316.5 9.7 %copy.102 = f32[2048,1024]{1,0:T(8,128)} copy(f32[2048,1024]{0,1:T(8,128)} %bitcast.173) | data formatting | bytes 16777216 | tf_op jit(solution)/shard_map/mul | solution.py:175
  326.1 12.9 %multiply_convert_fusion.3 = bf16[2048,1280]{1,0:T(8,128)(2,1)S(1)} fusion(bf16[2048,1280]{1,0:T(8,128)(2,1)} %copy-done.5, bf16[3,1280]{1,0:T(4,128)(2,1)S(1)} %collective-permute-done.3, f32[1280]{0:T(1024)S(1)} %get-tuple-element.33, f32[1280]{0:T(1024)S(1)} %get-tuple-element.34, f32[1280]{0:T(1024)S(1)} %get-tuple-element.32, ...), kind=kLoop, calls=%fused_computation.9 | loop fusion | flops 68157440 | bytes 10519040 | tf_op jit(solution)/shard_map/convert_element_type | solution.py:115
  344.1 11.6 %reshape.446 = bf16[8,256,16,64]{3,2,1,0:T(8,128)(2,1)} reshape(bf16[2048,1024]{1,0:T(8,128)(2,1)} %slice.227) | data formatting | bytes 8388608 | tf_op jit(solution)/shard_map/reshape | solution.py:116
  355.6 10.3 %copy.95 = bf16[8,256,16,64]{1,3,2,0:T(8,128)(2,1)} copy(bf16[8,256,16,64]{3,2,1,0:T(8,128)(2,1)} %reshape.446) | data formatting | bytes 8388608 | tf_op jit(solution)/shard_map/reshape | solution.py:116
  367.3 8.4 %fusion.7 = f32[8,16,128,64]{2,3,1,0:T(8,128)S(1)} fusion(bf16[8,256,16,64]{1,3,2,0:T(8,128)(2,1)} %copy.95, f32[8,256,128]{2,1,0:T(8,128)S(1)} %convert_element_type.99, f32[8,256,16]{1,2,0:T(8,128)S(1)} %get-tuple-element.56), kind=kOutput, calls=%fused_computation.10 | convolution fusion | flops 545259520 | bytes 9568256 | tf_op jit(solution)/shard_map/cjhn,cjhp->chnp/dot_general | solution.py:137
  380.2 4.3 collective-permute-start.4
  384.5 3.0 collective-permute-start.5
  396.8 12.9 %fusion.8 = f32[8,256,16,64]{1,3,2,0:T(8,128)} fusion(bf16[8,256,16,64]{1,3,2,0:T(8,128)(2,1)S(1)} %copy-done.9, f32[8,256,16,64]{1,3,2,0:T(8,128)S(1)} %bitcast.176, f32[16]{0:T(128)S(1)} %copy-done.39, f32[8,256,16]{1,2,0:T(8,128)S(1)} %copy-done.20, f32[8,16,256]{2,1,0:T(8,128)S(1)} %copy-done.19, f32[8,16,256]{2,1,0:T(8,128)S(1)} %copy-done.18, ...), kind=kOutput, calls=%fused_computation.12 | convolution fusion | flops 1134559232 | bytes 23527488 | tf_op jit(solution)/shard_map/chij,cjhp->cihp/dot_general | solution.py:131
  409.7 14.5 %copy.106 = f32[8,256,16,64]{3,2,1,0:T(8,128)} copy(f32[8,256,16,64]{1,3,2,0:T(8,128)} %fusion.8) | data formatting | bytes 16777216 | tf_op jit(solution)/shard_map/reshape;reshape | solution.py:174
  424.2 14.5 %reshape.445 = f32[2048,1024]{1,0:T(8,128)} reshape(f32[8,256,16,64]{3,2,1,0:T(8,128)} %copy.106) | data formatting | bytes 16777216 | tf_op jit(solution)/shard_map/reshape;reshape | solution.py:174
  440.7 10.6 %multiply_add_fusion = f32[2048,1024]{1,0:T(8,128)} fusion(f32[2048,1024]{1,0:T(8,128)} %reshape.445, f32[2048,1024]{1,0:T(8,128)} %copy.102, f32[130,1024]{1,0:T(8,128)S(1)} %convert_element_type.106, f32[130,1024]{1,0:T(8,128)S(1)} %convert_element_type.105, bf16[130,1024]{1,0:T(8,128)(2,1)} %collective-permute-done.6, f32[1024]{0:T(1024)S(1)} %bitcast.194, ...), kind=kOutput, calls=%fused_computation.13 | convolution fusion | flops 541851648 | bytes 27009024 | tf_op jit(solution)/shard_map/dot_general | solution.py:170
  451.3 10.2 %multiply_reduce_fusion.3 = (f32[512]{0:T(512)S(1)}, f32[512,1024]{1,0:T(8,128)S(1)}) fusion(bf16[512,4096]{1,0:T(8,128)(2,1)} %collective-permute-done.2, bf16[4096,1024]{1,0:T(8,128)(2,1)} %all-gather.5.cloned.1.call-done, f32[2048,1024]{1,0:T(8,128)} %multiply_add_fusion, s32[]{:T(128)S(6)} %select_n.65), kind=kOutput, calls=%fused_computation.57 | convolution fusion | flops 4299685376 | bytes 16779268 | tf_op jit(solution)/shard_map/dot_general | solution.py:182
  461.5 6.8 %multiply_reduce_fusion.2 = (f32[512]{0:T(512)S(1)}, f32[512,1024]{1,0:T(8,128)S(1)}) fusion(bf16[512,4096]{1,0:T(8,128)(2,1)} %collective-permute-done.1, bf16[4096,1024]{1,0:T(8,128)(2,1)S(1)} %copy-done.34, f32[2048,1024]{1,0:T(8,128)S(1)} %copy-done.6, s32[]{:T(128)S(6)} %select_n.64), kind=kOutput, calls=%fused_computation.55 | convolution fusion | flops 4299685376 | bytes 16779268 | tf_op jit(solution)/shard_map/dot_general | solution.py:182
  468.3 7.0 %multiply_reduce_fusion.1 = (f32[512]{0:T(512)S(1)}, f32[512,1024]{1,0:T(8,128)S(1)}) fusion(bf16[512,4096]{1,0:T(8,128)(2,1)} %collective-permute-done, bf16[4096,1024]{1,0:T(8,128)(2,1)S(1)} %copy-done.34, f32[2048,1024]{1,0:T(8,128)S(1)} %copy-done.6, s32[]{:T(128)S(6)} %select_n.63), kind=kOutput, calls=%fused_computation.53 | convolution fusion | flops 4299685376 | bytes 16779268 | tf_op jit(solution)/shard_map/dot_general | solution.py:182
  479.5 4.9 multiply_reduce_fusion
  484.4 18.6 %collective-permute-done.7 = bf16[512,1024]{1,0:T(8,128)(2,1)S(1)} collective-permute-done((bf16[512,1024]{1,0:T(8,128)(2,1)S(1)}, bf16[512,1024]{1,0:T(8,128)(2,1)S(1)}, u32[]{:S(2)}, u32[]{:S(2)}) %collective-permute-start.7) | collective-permute-done | bytes 1048608 | tf_op jit(solution)/shard_map/ppermute | solution.py:24
  503.7 17.3 %collective-permute-done.8 = bf16[512,1024]{1,0:T(8,128)(2,1)S(1)} collective-permute-done((bf16[512,1024]{1,0:T(8,128)(2,1)S(1)}, bf16[512,1024]{1,0:T(8,128)(2,1)S(1)}, u32[]{:S(2)}, u32[]{:S(2)}) %collective-permute-start.8) | collective-permute-done | bytes 1048608 | tf_op jit(solution)/shard_map/ppermute | solution.py:24
  (183 shorter events, 65.4 us)
Async XLA Ops:
  6.5 54.1 %copy-start = (f32[4,4096]{1,0:T(4,128)S(1)}, f32[4,4096]{1,0:T(4,128)}, u32[]{:S(2)}) copy-start(f32[4,4096]{1,0:T(4,128)} %param.18) | copy-start | bytes 196612
  6.5 228.0 %all-gather.3.cloned.1.call-start = ((), (), s32[]{:S(2)}) async-start(), calls=%async_computation.2 | async-start | bytes 13271040 | tf_op jit(solution)/shard_map/all_gather | solution.py:88
  48.9 9.0 %copy-start.37 = (f32[64]{0:T(128)S(1)}, f32[64]{0:T(128)}, u32[]{:S(2)}) copy-start(f32[64]{0:T(128)} %param.24) | copy-start | bytes 772
  48.9 11.8 %copy-start.38 = (f32[64]{0:T(128)S(1)}, f32[64]{0:T(128)}, u32[]{:S(2)}) copy-start(f32[64]{0:T(128)} %param.23) | copy-start | bytes 772
  49.0 195.5 %collective-permute-start = (bf16[512,4096]{1,0:T(8,128)(2,1)}, bf16[512,4096]{1,0:T(8,128)(2,1)}, u32[]{:S(2)}, u32[]{:S(2)}) collective-permute-start(bf16[512,4096]{1,0:T(8,128)(2,1)} %param.13), channel_id=1, source_target_pairs={{0,2},{2,0},{4,6},{6,4},{8,10},{10,8},{12,14},{14,12},{16,18},{18,... | collective-permute-start | bytes 12582920 | tf_op jit(solution)/shard_map/ppermute | solution.py:24
  52.1 113.1 %all-to-all-start.1 = ((bf16[4,256,1024]{1,2,0:T(8,128)(2,1)}), bf16[4,256,1024]{1,2,0:T(8,128)(2,1)S(1)}, u32[]{:S(2)}, u32[]{:S(2)}) async-start(bf16[4,256,1024]{1,2,0:T(8,128)(2,1)} %bitcast.178), calls=%async_computation.1 | async-start | bytes 4194304 | tf_op jit(solution)/shard_map/all_to_all | solution.py:16
  55.8 395.5 %all-gather.5.cloned.1.call-start = ((), (), s32[]{:S(2)}) async-start(), calls=%async_computation.3 | async-start | bytes 10485760 | tf_op jit(solution)/shard_map/all_gather | solution.py:91
  55.9 203.1 %collective-permute-start.1 = (bf16[512,4096]{1,0:T(8,128)(2,1)}, bf16[512,4096]{1,0:T(8,128)(2,1)}, u32[]{:S(2)}, u32[]{:S(2)}) collective-permute-start(bf16[512,4096]{1,0:T(8,128)(2,1)} %param.13), channel_id=1, source_target_pairs={{0,4},{2,6},{4,0},{6,2},{8,12},{10,14},{12,8},{14,10},{16,20},{18,... | collective-permute-start | bytes 12582920 | tf_op jit(solution)/shard_map/ppermute | solution.py:24
  61.6 206.5 %collective-permute-start.2 = (bf16[512,4096]{1,0:T(8,128)(2,1)}, bf16[512,4096]{1,0:T(8,128)(2,1)}, u32[]{:S(2)}, u32[]{:S(2)}) collective-permute-start(bf16[512,4096]{1,0:T(8,128)(2,1)} %param.13), channel_id=1, source_target_pairs={{0,6},{2,4},{4,2},{6,0},{8,14},{10,12},{12,10},{14,8},{16,22},{18,... | collective-permute-start | bytes 12582920 | tf_op jit(solution)/shard_map/ppermute | solution.py:24
  234.6 9.9 %copy-start.33 = (bf16[4096,1296]{0,1:T(8,128)(2,1)S(1)}, bf16[4096,1296]{0,1:T(8,128)(2,1)}, u32[]{:S(2)}) copy-start(bf16[4096,1296]{0,1:T(8,128)(2,1)} %all-gather.3.cloned.1.call-done) | copy-start | bytes 31850500
  244.4 10.2 %copy-start.13 = (f32[512,1296]{0,1:T(8,128)}, f32[512,1296]{0,1:T(8,128)S(1)}, u32[]{:S(2)}) copy-start(f32[512,1296]{0,1:T(8,128)S(1)} %fusion.65) | copy-start | bytes 7962628
  254.6 13.5 %copy-start.14 = (f32[512,1296]{0,1:T(8,128)}, f32[512,1296]{0,1:T(8,128)S(1)}, u32[]{:S(2)}) copy-start(f32[512,1296]{0,1:T(8,128)S(1)} %fusion.66) | copy-start | bytes 7962628
  268.1 10.0 %copy-start.15 = (f32[512,1296]{0,1:T(8,128)}, f32[512,1296]{0,1:T(8,128)S(1)}, u32[]{:S(2)}) copy-start(f32[512,1296]{0,1:T(8,128)S(1)} %fusion.67) | copy-start | bytes 7962628
  286.2 89.5 %copy-start.24 = (f32[16]{0:T(128)}, f32[16]{0:T(128)S(1)}, u32[]{:S(2)}) copy-start(f32[16]{0:T(128)S(1)} %get-tuple-element.27) | copy-start | bytes 196
  286.2 89.5 %copy-start.26 = (f32[16]{0:T(128)}, f32[16]{0:T(128)S(1)}, u32[]{:S(2)}) copy-start(f32[16]{0:T(128)S(1)} %get-tuple-element.23) | copy-start | bytes 196
  286.2 89.5 %copy-start.28 = (f32[16]{0:T(128)}, f32[16]{0:T(128)S(1)}, u32[]{:S(2)}) copy-start(f32[16]{0:T(128)S(1)} %get-tuple-element.28) | copy-start | bytes 196
  306.9 19.3 %collective-permute-start.3 = (bf16[3,1280]{1,0:T(4,128)(2,1)S(1)}, bf16[3,1280]{1,0:T(4,128)(2,1)S(1)}, u32[]{:S(2)}, u32[]{:S(2)}) collective-permute-start(bf16[3,1280]{1,0:T(4,128)(2,1)S(1)} %slice.218), channel_id=1, source_target_pairs={{0,8},{2,10},{4,12},{6,14},{8,16},{10,18},{12,20},{14,22},{16,24},... | collective-permute-start | bytes 23048 | tf_op jit(solution)/shard_map/ppermute | solution.py:104
  367.3 10.5 %copy-start.29 = (f32[16]{0:T(128)S(1)}, f32[16]{0:T(128)}, u32[]{:S(2)}) copy-start(f32[16]{0:T(128)} %get-tuple-element.24) | copy-start | bytes 196
  367.3 10.5 %copy-start.30 = (f32[16]{0:T(128)S(1)}, f32[16]{0:T(128)}, u32[]{:S(2)}) copy-start(f32[16]{0:T(128)} %get-tuple-element.26) | copy-start | bytes 196
  367.3 10.5 %copy-start.32 = (f32[16]{0:T(128)S(1)}, f32[16]{0:T(128)}, u32[]{:S(2)}) copy-start(f32[16]{0:T(128)} %get-tuple-element.15) | copy-start | bytes 196
  375.7 13.8 %copy-start.11 = (bf16[8,16,128,64]{2,3,1,0:T(8,128)(2,1)S(1)}, bf16[8,16,128,64]{2,3,1,0:T(8,128)(2,1)}, u32[]{:S(2)}) copy-start(bf16[8,16,128,64]{2,3,1,0:T(8,128)(2,1)} %broadcast_dynamic-update-slice_fusion) | copy-start | bytes 6291460
  378.2 15.1 %copy-start.25 = (f32[16]{0:T(128)S(1)}, f32[16]{0:T(128)}, u32[]{:S(2)}) copy-start(f32[16]{0:T(128)} %copy-done.24) | copy-start | bytes 196
  379.1 14.2 %copy-start.4 = (f32[8,16,128,64]{2,3,1,0:T(8,128)S(1)}, f32[8,16,128,64]{2,3,1,0:T(8,128)}, u32[]{:S(2)}) copy-start(f32[8,16,128,64]{2,3,1,0:T(8,128)} %copy-done.3) | copy-start | bytes 12582916
  380.2 58.4 %collective-permute-start.4 = (bf16[130,1024]{1,0:T(8,128)(2,1)S(1)}, bf16[130,1024]{1,0:T(8,128)(2,1)}, u32[]{:S(2)}, u32[]{:S(2)}) collective-permute-start(bf16[130,1024]{1,0:T(8,128)(2,1)S(1)} %pad_maximum_fusion.1), channel_id=1, source_target_pairs={{0,8},{2,10},{4,12},{6,14},{8,16},{10,18},{12,20},{14,22},{16,24},... | collective-permute-start | bytes 798728 | tf_op jit(solution)/shard_map/ppermute | solution.py:31
  384.5 55.2 %collective-permute-start.5 = (bf16[130,1024]{1,0:T(8,128)(2,1)S(1)}, bf16[130,1024]{1,0:T(8,128)(2,1)}, u32[]{:S(2)}, u32[]{:S(2)}) collective-permute-start(bf16[130,1024]{1,0:T(8,128)(2,1)S(1)} %pad_maximum_fusion.1), channel_id=1, source_target_pairs={{0,16},{2,18},{4,20},{6,22},{8,24},{10,26},{12,28},{14,30},{1,17},... | collective-permute-start | bytes 798728 | tf_op jit(solution)/shard_map/ppermute | solution.py:31
  387.6 53.2 %collective-permute-start.6 = (bf16[130,1024]{1,0:T(8,128)(2,1)S(1)}, bf16[130,1024]{1,0:T(8,128)(2,1)}, u32[]{:S(2)}, u32[]{:S(2)}) collective-permute-start(bf16[130,1024]{1,0:T(8,128)(2,1)S(1)} %pad_maximum_fusion.1), channel_id=1, source_target_pairs={{0,24},{2,26},{4,28},{6,30},{1,25},{3,27},{5,29},{7,31}} | collective-permute-start | bytes 798728 | tf_op jit(solution)/shard_map/ppermute | solution.py:31
  451.3 10.2 %copy-start.6 = (f32[2048,1024]{1,0:T(8,128)S(1)}, f32[2048,1024]{1,0:T(8,128)}, u32[]{:S(2)}) copy-start(f32[2048,1024]{1,0:T(8,128)} %multiply_add_fusion) | copy-start | bytes 25165828
  451.3 10.2 %copy-start.34 = (bf16[4096,1024]{1,0:T(8,128)(2,1)S(1)}, bf16[4096,1024]{1,0:T(8,128)(2,1)}, u32[]{:S(2)}) copy-start(bf16[4096,1024]{1,0:T(8,128)(2,1)} %all-gather.5.cloned.1.call-done) | copy-start | bytes 25165828
  476.0 27.1 %collective-permute-start.7 = (bf16[512,1024]{1,0:T(8,128)(2,1)S(1)}, bf16[512,1024]{1,0:T(8,128)(2,1)S(1)}, u32[]{:S(2)}, u32[]{:S(2)}) collective-permute-start(bf16[512,1024]{1,0:T(8,128)(2,1)S(1)} %get-tuple-element.61), channel_id=1, source_target_pairs={{0,6},{2,4},{4,2},{6,0},{8,14},{10,12},{12,10},{14,8},{16,22},{18,... | collective-permute-start | bytes 3145736 | tf_op jit(solution)/shard_map/ppermute | solution.py:24
  477.4 43.5 %collective-permute-start.8 = (bf16[512,1024]{1,0:T(8,128)(2,1)S(1)}, bf16[512,1024]{1,0:T(8,128)(2,1)S(1)}, u32[]{:S(2)}, u32[]{:S(2)}) collective-permute-start(bf16[512,1024]{1,0:T(8,128)(2,1)S(1)} %get-tuple-element.60), channel_id=1, source_target_pairs={{0,4},{2,6},{4,0},{6,2},{8,12},{10,14},{12,8},{14,10},{16,20},{18,... | collective-permute-start | bytes 3145736 | tf_op jit(solution)/shard_map/ppermute | solution.py:24
  478.9 42.1 %collective-permute-start.9 = (bf16[512,1024]{1,0:T(8,128)(2,1)S(1)}, bf16[512,1024]{1,0:T(8,128)(2,1)S(1)}, u32[]{:S(2)}, u32[]{:S(2)}) collective-permute-start(bf16[512,1024]{1,0:T(8,128)(2,1)S(1)} %get-tuple-element.59), channel_id=1, source_target_pairs={{0,2},{2,0},{4,6},{6,4},{8,10},{10,8},{12,14},{14,12},{16,18},{18,... | collective-permute-start | bytes 3145736 | tf_op jit(solution)/shard_map/ppermute | solution.py:24
  503.5 20.9 %copy-start.1 = (f32[4,4096]{1,0:T(4,128)S(1)}, f32[4,4096]{1,0:T(4,128)}, u32[]{:S(2)}) copy-start(f32[4,4096]{1,0:T(4,128)} %param.18) | copy-start | bytes 196612
  (21 other events, 75.3 us)
Sparse Core Ops, SparseCore 0:
  49.0 185.5 all-gather.2
  236.1 147.8 all-gather.4

commit v3 on v2

--- a/solution.py
+++ b/solution.py
@@ -1,6 +1,10 @@
+import functools
+
 import jax
 import jax.numpy as jnp
 from jax import lax
+from jax.experimental import pallas as pl
+from jax.experimental.pallas import tpu as pltpu
 from jax.sharding import PartitionSpec as P
 
 SPAN = 256
@@ -37,6 +41,85 @@
                 everyone, jnp.maximum(level - back, 0), keepdims=False
             )
             yield jnp.where(back <= level, part, 0)
+
+
+def scan_body(
+    width, state_size, conv, cumul, cumul_t, step_t, ending, decay, skip, out, state
+):
+    @pl.when(pl.program_id(0) == 0)
+    def _():
+        state[...] = jnp.zeros_like(state)
+
+    b_in = conv[:, width : width + state_size]
+    c_in = conv[:, width + state_size :]
+    scores = lax.dot_general(
+        c_in, b_in, (((1,), (1,)), ((), ())), preferred_element_type=F32
+    )
+    row = lax.broadcasted_iota(jnp.int32, (SPAN, SPAN), 0)
+    col = lax.broadcasted_iota(jnp.int32, (SPAN, SPAN), 1)
+    scores = jnp.where(row >= col, scores, 0.0)
+    first = lax.broadcasted_iota(jnp.int32, (SPAN, 128), 1) < 64
+    for pair in range(width // 128):
+        lanes = slice(pair * 128, pair * 128 + 128)
+        x_in = conv[:, lanes]
+        x_wide = x_in.astype(F32)
+        sums = []
+        for head in (2 * pair, 2 * pair + 1):
+            gap = cumul[:, head : head + 1] - cumul_t[0, head : head + 1, :]
+            weight = scores * jnp.exp(jnp.minimum(gap, 0.0)) * step_t[0, head : head + 1, :]
+            sums.append(jnp.dot(weight.astype(BF16), x_in, preferred_element_type=F32))
+
+        def both(ref):
+            return jnp.where(
+                first, ref[:, 2 * pair : 2 * pair + 1], ref[:, 2 * pair + 1 : 2 * pair + 2]
+            )
+
+        old = state[:, lanes]
+        inter = jnp.dot(c_in, old.astype(BF16), preferred_element_type=F32)
+        out[:, lanes] = (
+            jnp.where(first, sums[0], sums[1])
+            + inter * jnp.exp(both(cumul))
+            + skip[:, lanes] * x_wide
+        )
+        scaled = (x_wide * both(ending)).astype(BF16)
+        new = lax.dot_general(
+            b_in, scaled, (((0,), (0,)), ((), ())), preferred_element_type=F32
+        )
+        state[:, lanes] = decay[0, :, lanes] * old + new
+
+
+def local_scan(
+    conv, cumul, cumul_t, step_t, ending, decay, skip, width, state_size, heads
+):
+    rows = conv.shape[0]
+    return pl.pallas_call(
+        functools.partial(scan_body, width, state_size),
+        grid=(rows // SPAN,),
+        in_specs=[
+            pl.BlockSpec((SPAN, conv.shape[1]), lambda i: (i, 0)),
+            pl.BlockSpec((SPAN, heads), lambda i: (i, 0)),
+            pl.BlockSpec((1, heads, SPAN), lambda i: (i, 0, 0)),
+            pl.BlockSpec((1, heads, SPAN), lambda i: (i, 0, 0)),
+            pl.BlockSpec((SPAN, heads), lambda i: (i, 0)),
+            pl.BlockSpec((1, 1, width), lambda i: (i, 0, 0)),
+            pl.BlockSpec((1, width), lambda i: (0, 0)),
+        ],
+        out_specs=[
+            pl.BlockSpec((SPAN, width), lambda i: (i, 0)),
+            pl.BlockSpec((state_size, width), lambda i: (0, 0)),
+        ],
+        out_shape=[
+            jax.ShapeDtypeStruct((rows, width), F32),
+            jax.ShapeDtypeStruct((state_size, width), F32),
+        ],
+        compiler_params=pltpu.CompilerParams(vmem_limit_bytes=32 * 1024 * 1024),
+        cost_estimate=pl.CostEstimate(
+            flops=2 * rows * width * (SPAN + 2 * state_size),
+            bytes_accessed=rows * width * 8,
+            transcendentals=rows * SPAN * heads,
+        ),
+        name="local_scan",
+    )(conv, cumul, cumul_t, step_t, ending, decay, skip)
 
 
 def on_device(
@@ -113,51 +196,36 @@
     for tap in range(kernel):
         running = running + taps[tap][None, :] * extended[tap : tap + rows].astype(F32)
     conv = jax.nn.silu(running).astype(BF16)
-    inner = conv[:, :width].reshape(blocks, SPAN, heads, head_dim)
-    b_in = conv[:, width : width + state_size].reshape(blocks, SPAN, state_size)
-    c_in = conv[:, width + state_size :].reshape(blocks, SPAN, state_size)
-
     step = jax.nn.softplus(step_sum + take(dt_bias)[None, :])
     log_rate = -jnp.exp(take(a_log))[None, :] * step
     cumul = jnp.cumsum(log_rate.reshape(blocks, SPAN, heads), axis=1)
     step = step.reshape(blocks, SPAN, heads)
-    scores = jnp.einsum("cin,cjn->cij", c_in, b_in, preferred_element_type=F32)
-    cumul_t = jnp.swapaxes(cumul, 1, 2)
-    step_t = jnp.swapaxes(step, 1, 2)
-    gap = cumul_t[:, :, :, None] - cumul_t[:, :, None, :]
-    causal = jnp.arange(SPAN)[:, None] >= jnp.arange(SPAN)[None, :]
-    decay = jnp.where(causal[None, None], jnp.exp(jnp.minimum(gap, 0.0)), 0.0)
-    weight = (scores[:, None] * decay * step_t[:, :, None, :]).astype(BF16)
-    intra = jnp.einsum("chij,cjhp->cihp", weight, inner, preferred_element_type=F32)
     block_log = cumul[:, -1, :]
-    weighted_b = (
-        (jnp.exp(block_log[:, None, :] - cumul) * step)[..., None]
-        * b_in[:, :, None, :].astype(F32)
-    ).astype(BF16)
-    local = jnp.einsum("cjhn,cjhp->chnp", weighted_b, inner, preferred_element_type=F32)
-    state = jnp.zeros((heads, state_size, head_dim), F32)
-    before = jnp.zeros((heads,), F32)
-    starts, befores = [], []
-    for block in range(blocks):
-        starts.append(state)
-        befores.append(before)
-        state = jnp.exp(block_log[block])[:, None, None] * state + local[block]
-        before = before + block_log[block]
-    starts = jnp.stack(starts).astype(BF16)
-    inter = jnp.einsum("cin,chnp->cihp", c_in, starts, preferred_element_type=F32)
-    scan = (
-        intra
-        + inter * jnp.exp(cumul)[..., None]
-        + take(d_skip)[None, None, :, None] * inner.astype(F32)
-    ).reshape(rows, width)
-    reach = jnp.exp(cumul + jnp.stack(befores)[:, None, :]).reshape(rows, heads)
+    ending = (jnp.exp(block_log[:, None, :] - cumul) * step).reshape(rows, heads)
+    before = jnp.cumsum(block_log, axis=0)
+    reach = jnp.exp(cumul + (before - block_log)[:, None, :]).reshape(rows, heads)
+    before = before[-1]
+    scan, state = local_scan(
+        conv,
+        cumul.reshape(rows, heads),
+        jnp.swapaxes(cumul, 1, 2),
+        jnp.swapaxes(step, 1, 2),
+        ending,
+        jnp.repeat(jnp.exp(block_log), head_dim, axis=1)[:, None, :],
+        jnp.repeat(take(d_skip), head_dim)[None, :],
+        width,
+        state_size,
+        heads,
+    )
+    spread = jnp.repeat(jnp.eye(heads, dtype=F32), head_dim, axis=1)
+    reach = jnp.dot(reach, spread, precision=lax.Precision.HIGHEST)
 
     high = lax.reduce_precision(before, 8, 7)
     low = before - high
     logs = jnp.stack([high, low]).astype(BF16)
     packed = jnp.concatenate(
         [
-            state.transpose(1, 0, 2).reshape(state_size, width).astype(BF16),
+            state.astype(BF16),
             jnp.repeat(logs, head_dim, axis=1),
         ]
     )
@@ -168,12 +236,9 @@
         carried = carried + jnp.exp(skipped)[None, :] * part[:state_size]
         skipped = skipped + part[state_size] + part[state_size + 1]
     far = jnp.dot(
-        c_in.reshape(rows, state_size), carried.astype(BF16), preferred_element_type=F32
-    )
-    scan = (
-        scan.reshape(rows, heads, head_dim)
-        + far.reshape(rows, heads, head_dim) * reach[:, :, None]
-    ).reshape(rows, width)
+        conv[:, width + state_size :], carried.astype(BF16), preferred_element_type=F32
+    )
+    scan = scan + far * reach
 
     scan, w_gate = lax.optimization_barrier((scan, w_gate))
     gain = take(norm_gain)[None, :]

time: 542 us -> 497 us (0.917)
  the two profiles are of different devices: /device:TPU:0 before, /device:TPU:27 now
where the time goes in v3:
time: 497 us; the launch traced here: 488 us
  waiting for transfers between devices  275 us (55%)
  matrix products  78 us (16%)
  blocking collectives  32.9 us (7%)
  local copies, waits for them, and re-layouts  28.6 us (6%)
  other arithmetic  27.4 us (6%)
  Pallas kernels  16.7 us (3%)
  starting transfers between devices  14.7 us (3%)
  between operations  14.3 us (3%)
    all_to_all x1, waiting for transfers between devices, exchange_columns(): lax.all_to_all(parts.swapaxes(0, 1), 'ctx', 0, 0, axis_index_groups=group...  102 us
    all_gather x1, waiting for transfers between devices, on_device(): lax.all_gather(main, 'ctx', axis=0, tiled=True, axis_index_groups=along)  69.1 us
    ppermute x6, waiting for transfers between devices, swapped(): return lax.ppermute(value, 'ctx', pairs)  45.6 us
    ppermute x3, waiting for transfers between devices, earlier_parts(): yield lax.ppermute(value, 'ctx', pairs)  39.8 us
    dot_general x4, matrix products, on_device(): projected = jnp.dot(piece, main, preferred_element_type=F32)  37.5 us
    all_to_all x1, blocking collectives, exchange_columns(): lax.all_to_all(parts.swapaxes(0, 1), 'ctx', 0, 0, axis_index_groups=group...  32.9 us
    dot_general x4, matrix products, on_device(): jnp.dot(pieces[step], w_gate, preferred_element_type=F32).astype(BF16)  29.1 us
    pallas_call x1, Pallas kernels, local_scan(): pl.pallas_call(functools.partial(scan_body, width, state_size), grid=(row...  16.7 us
  transfers between devices with their start and end apart: 13, of which 9 were waited for; matrix products, arithmetic and copies ran while one was open for 20% of the time, Pallas kernels for 3%

profile of v3, /device:TPU:27, one launch (start us, length us, event | category | flops | bytes accessed | tf_op | source)
XLA Modules:
  0.0 487.5 jit_solution(2157938517698978129)
XLA Ops:
  6.5 3.3 copy.83
  10.4 32.9 %all_to_all.10 = bf16[4,256,1296]{1,2,0:T(8,128)(2,1)S(1)} all-to-all(bf16[4,256,1296]{1,2,0:T(8,128)(2,1)S(1)} %maximum_bitcast_fusion), channel_id=1, replica_groups={{0,2,4,6},{8,10,12,14},{16,18,20,22},{24,26,28,30},{1,3,5,7},{9,11,13,1..., dimensions={0} | all-to-all | bytes 5308416 | tf_op jit(solution)/shard_map/all_to_all | solution.py:20
  43.3 1.9 copy.113
  46.6 2.5 copy.102
  49.0 3.8 all-to-all-start.1
  56.4 102.3 %all-to-all-done.1 = bf16[4,256,1024]{1,2,0:T(8,128)(2,1)S(1)} async-done(((bf16[4,256,1024]{1,2,0:T(8,128)(2,1)}), bf16[4,256,1024]{1,2,0:T(8,128)(2,1)S(1)}, u32[]{:S(2)}, u32[]{:S(2)}) %all-to-all-start.1) | async-done | bytes 2097184 | tf_op jit(solution)/shard_map/all_to_all | solution.py:20
  158.6 2.4 copy.103
  161.1 69.1 %all-gather.3.cloned.1.call-done = bf16[4096,1296]{0,1:T(8,128)(2,1)} async-done(((bf16[1024,1296]{0,1:T(8,128)(2,1)}), bf16[4096,1296]{0,1:T(8,128)(2,1)}) %all-gather.3.cloned.1.call-update) | async-done | bytes 10616848 | tf_op jit(solution)/shard_map/all_gather | solution.py:171
  230.2 9.8 %fusion.42 = f32[512,1296]{0,1:T(8,128)S(1)} fusion(bf16[512,4096]{1,0:T(8,128)(2,1)} %param.13, bf16[4096,1296]{0,1:T(8,128)(2,1)} %all-gather.3.cloned.1.call-done), kind=kOutput, calls=%fused_computation.117 | convolution fusion | flops 5435817984 | bytes 17465344 | tf_op jit(solution)/shard_map/dot_general | solution.py:181
  240.1 9.3 %fusion.43 = f32[512,1296]{0,1:T(8,128)S(1)} fusion(bf16[512,4096]{1,0:T(8,128)(2,1)} %collective-permute-done, bf16[4096,1296]{0,1:T(8,128)(2,1)S(1)} %copy-done.12), kind=kOutput, calls=%fused_computation.118 | convolution fusion | flops 5435817984 | bytes 17465344 | tf_op jit(solution)/shard_map/dot_general | solution.py:181
  249.4 5.4 %collective-permute-done.1 = bf16[512,4096]{1,0:T(8,128)(2,1)} collective-permute-done((bf16[512,4096]{1,0:T(8,128)(2,1)}, bf16[512,4096]{1,0:T(8,128)(2,1)}, u32[]{:S(2)}, u32[]{:S(2)}) %collective-permute-start.1) | collective-permute-done | bytes 4194336 | tf_op jit(solution)/shard_map/ppermute | solution.py:28
  254.8 9.1 %fusion.44 = f32[512,1296]{0,1:T(8,128)S(1)} fusion(bf16[512,4096]{1,0:T(8,128)(2,1)} %collective-permute-done.1, bf16[4096,1296]{0,1:T(8,128)(2,1)S(1)} %copy-done.12), kind=kOutput, calls=%fused_computation.119 | convolution fusion | flops 5435817984 | bytes 17465344 | tf_op jit(solution)/shard_map/dot_general | solution.py:181
  265.5 9.3 %fusion.45 = f32[512,1296]{0,1:T(8,128)S(1)} fusion(bf16[512,4096]{1,0:T(8,128)(2,1)} %collective-permute-done.2, bf16[4096,1296]{0,1:T(8,128)(2,1)S(1)} %copy-done.12), kind=kOutput, calls=%fused_computation.120 | convolution fusion | flops 5435817984 | bytes 17465344 | tf_op jit(solution)/shard_map/dot_general | solution.py:181
  276.3 4.6 reduce-window.6
  281.6 2.4 copy.106
  293.2 1.7 collective-permute-done.3
  295.0 12.5 %multiply_convert_fusion.conv = bf16[2048,1280]{1,0:T(8,128)(2,1)S(1)} fusion(bf16[2048,1280]{1,0:T(8,128)(2,1)} %copy-done.2, bf16[3,1280]{1,0:T(4,128)(2,1)S(1)} %collective-permute-done.3, f32[1280]{0:T(1024)S(1)} %get-tuple-element.21, f32[1280]{0:T(1024)S(1)} %get-tuple-element.22, f32[1280]{0:T(1024)S(1)} %get-tuple-element.20, ...), kind=kLoop, calls=%fused_computation | loop fusion | flops 68157440 | bytes 10519040 | tf_op jit(solution)/shard_map/convert_element_type | solution.py:198
  307.5 16.7 %local_scan.1 = (f32[2048,1024]{1,0:T(8,128)S(1)}, f32[128,1024]{1,0:T(8,128)S(1)}) custom-call(bf16[2048,1280]{1,0:T(8,128)(2,1)S(1)} %multiply_convert_fusion.conv, f32[2048,16]{1,0:T(8,128)S(1)} %bitcast.77, f32[8,16,256]{2,1,0:T(8,128)S(1)} %get-tuple-element.29.cumul_t, f32[8,16,256]{2,1,0:T(8,128)S(1)} %bitcast.79, f32[2048,16]{1,0:T(8,128)S(1)} %bitcast.78, ...), custom_call_target="tpu_custom_call" | custom-call | flops 2147483648 | bytes 16777216 | tf_op jit(solution)/shard_map/local_scan/pallas_call | solution.py:95
  326.8 1.7 collective-permute-start.6
  328.5 6.8 %fusion.46 = f32[2048,1024]{1,0:T(8,128)S(1)} fusion(f32[2048,16]{0,1:T(8,128)S(1)} %bitcast.87, f32[16,1024]{1,0:T(8,128)S(1)} %reshape.103), kind=kOutput, calls=%fused_computation.121 | convolution fusion | flops 402653184 | bytes 8585216 | tf_op jit(solution)/shard_map/dot_general | solution.py:221
  335.4 11.3 %collective-permute-done.4 = bf16[130,1024]{1,0:T(8,128)(2,1)S(1)} collective-permute-done((bf16[130,1024]{1,0:T(8,128)(2,1)S(1)}, bf16[130,1024]{1,0:T(8,128)(2,1)S(1)}, u32[]{:S(2)}, u32[]{:S(2)}) %collective-permute-start.4) | collective-permute-done | bytes 266272 | tf_op jit(solution)/shard_map/ppermute | solution.py:35
  346.7 28.6 %collective-permute-done.5 = bf16[130,1024]{1,0:T(8,128)(2,1)S(1)} collective-permute-done((bf16[130,1024]{1,0:T(8,128)(2,1)S(1)}, bf16[130,1024]{1,0:T(8,128)(2,1)S(1)}, u32[]{:S(2)}, u32[]{:S(2)}) %collective-permute-start.5) | collective-permute-done | bytes 266272 | tf_op jit(solution)/shard_map/ppermute | solution.py:35
  375.4 4.5 fusion.22
  379.9 7.4 %multiply_add_fusion = f32[2048,1024]{1,0:T(8,128)} fusion(f32[2048,1024]{1,0:T(8,128)S(1)} %get-tuple-element.14, f32[2048,1024]{1,0:T(8,128)} %fusion.22, f32[2048,1024]{1,0:T(8,128)S(1)} %fusion.46), kind=kLoop, calls=%fused_computation.1 | loop fusion | flops 4194304 | bytes 33554432 | tf_op jit(solution)/shard_map/add | solution.py:241
  387.2 16.4 %all-gather.5.cloned.1.call-done = bf16[4096,1024]{1,0:T(8,128)(2,1)} async-done(((bf16[1024,1024]{1,0:T(8,128)(2,1)}), bf16[4096,1024]{1,0:T(8,128)(2,1)}) %all-gather.5.cloned.1.call-update) | async-done | bytes 8388624 | tf_op jit(solution)/shard_map/all_gather | solution.py:174
  403.6 10.2 %multiply_reduce_fusion.3 = (f32[512]{0:T(512)S(1)}, f32[512,1024]{1,0:T(8,128)S(1)}) fusion(bf16[512,4096]{1,0:T(8,128)(2,1)} %collective-permute-done.2, bf16[4096,1024]{1,0:T(8,128)(2,1)} %all-gather.5.cloned.1.call-done, f32[2048,1024]{1,0:T(8,128)} %multiply_add_fusion, s32[]{:T(128)S(6)} %select_n.61), kind=kOutput, calls=%fused_computation.43 | convolution fusion | flops 4299685376 | bytes 16779268 | tf_op jit(solution)/shard_map/dot_general | solution.py:247
  413.8 6.9 %multiply_reduce_fusion.2 = (f32[512]{0:T(512)S(1)}, f32[512,1024]{1,0:T(8,128)S(1)}) fusion(bf16[512,4096]{1,0:T(8,128)(2,1)} %collective-permute-done.1, bf16[4096,1024]{1,0:T(8,128)(2,1)S(1)} %copy-done.13, f32[2048,1024]{1,0:T(8,128)S(1)} %copy-done.3, s32[]{:T(128)S(6)} %select_n.60), kind=kOutput, calls=%fused_computation.41 | convolution fusion | flops 4299685376 | bytes 16779268 | tf_op jit(solution)/shard_map/dot_general | solution.py:247
  420.7 7.1 %multiply_reduce_fusion.1 = (f32[512]{0:T(512)S(1)}, f32[512,1024]{1,0:T(8,128)S(1)}) fusion(bf16[512,4096]{1,0:T(8,128)(2,1)} %collective-permute-done, bf16[4096,1024]{1,0:T(8,128)(2,1)S(1)} %copy-done.13, f32[2048,1024]{1,0:T(8,128)S(1)} %copy-done.3, s32[]{:T(128)S(6)} %select_n.59), kind=kOutput, calls=%fused_computation.39 | convolution fusion | flops 4299685376 | bytes 16779268 | tf_op jit(solution)/shard_map/dot_general | solution.py:247
  431.2 5.0 %multiply_reduce_fusion = (f32[512]{0:T(512)S(1)}, f32[512,1024]{1,0:T(8,128)S(1)}) fusion(bf16[512,4096]{1,0:T(8,128)(2,1)S(1)} %copy-done.14, bf16[4096,1024]{1,0:T(8,128)(2,1)S(1)} %copy-done.13, f32[2048,1024]{1,0:T(8,128)S(1)} %copy-done.3, s32[]{:T(128)S(6)} %select_n.58), kind=kOutput, calls=%fused_computation.37 | convolution fusion | flops 4299685376 | bytes 16779268 | tf_op jit(solution)/shard_map/dot_general | solution.py:247
  436.2 17.6 %collective-permute-done.7 = bf16[512,1024]{1,0:T(8,128)(2,1)S(1)} collective-permute-done((bf16[512,1024]{1,0:T(8,128)(2,1)S(1)}, bf16[512,1024]{1,0:T(8,128)(2,1)S(1)}, u32[]{:S(2)}, u32[]{:S(2)}) %collective-permute-start.7) | collective-permute-done | bytes 1048608 | tf_op jit(solution)/shard_map/ppermute | solution.py:28
  454.4 22.6 %collective-permute-done.8 = bf16[512,1024]{1,0:T(8,128)(2,1)S(1)} collective-permute-done((bf16[512,1024]{1,0:T(8,128)(2,1)S(1)}, bf16[512,1024]{1,0:T(8,128)(2,1)S(1)}, u32[]{:S(2)}, u32[]{:S(2)}) %collective-permute-start.8) | collective-permute-done | bytes 1048608 | tf_op jit(solution)/shard_map/ppermute | solution.py:28
  477.3 2.0 copy-done.6
  (127 shorter events, 26.3 us)
Async XLA Ops:
  6.5 49.5 %copy-start = (f32[4,4096]{1,0:T(4,128)S(1)}, f32[4,4096]{1,0:T(4,128)}, u32[]{:S(2)}) copy-start(f32[4,4096]{1,0:T(4,128)} %param.18) | copy-start | bytes 196612
  6.5 3.4 copy-start.8
  6.5 3.7 copy-start.9
  6.5 223.7 %all-gather.3.cloned.1.call-start = ((), (), s32[]{:S(2)}) async-start(), calls=%async_computation.2 | async-start | bytes 13271040 | tf_op jit(solution)/shard_map/all_gather | solution.py:171
  43.3 3.3 copy-start.7
  45.2 8.8 %copy-start.10 = (f32[4,4,256]{2,1,0:T(4,128)S(1)}, f32[4,4,256]{2,1,0:T(4,128)}, u32[]{:S(2)}) copy-start(f32[4,4,256]{2,1,0:T(4,128)} %param.19) | copy-start | bytes 49156
  45.2 8.8 %copy-start.11 = (f32[4,256]{1,0:T(4,128)S(1)}, f32[4,256]{1,0:T(4,128)}, u32[]{:S(2)}) copy-start(f32[4,256]{1,0:T(4,128)} %param.21) | copy-start | bytes 12292
  45.2 8.8 %copy-start.15 = (f32[64]{0:T(128)S(1)}, f32[64]{0:T(128)}, u32[]{:S(2)}) copy-start(f32[64]{0:T(128)} %param.22) | copy-start | bytes 772
  45.2 8.9 %copy-start.16 = (f32[64]{0:T(128)S(1)}, f32[64]{0:T(128)}, u32[]{:S(2)}) copy-start(f32[64]{0:T(128)} %param.24) | copy-start | bytes 772
  45.2 10.9 %copy-start.17 = (f32[64]{0:T(128)S(1)}, f32[64]{0:T(128)}, u32[]{:S(2)}) copy-start(f32[64]{0:T(128)} %param.23) | copy-start | bytes 772
  45.3 194.8 %collective-permute-start = (bf16[512,4096]{1,0:T(8,128)(2,1)}, bf16[512,4096]{1,0:T(8,128)(2,1)}, u32[]{:S(2)}, u32[]{:S(2)}) collective-permute-start(bf16[512,4096]{1,0:T(8,128)(2,1)} %param.13), channel_id=1, source_target_pairs={{0,2},{2,0},{4,6},{6,4},{8,10},{10,8},{12,14},{14,12},{16,18},{18,... | collective-permute-start | bytes 12582920 | tf_op jit(solution)/shard_map/ppermute | solution.py:28
  49.0 109.6 %all-to-all-start.1 = ((bf16[4,256,1024]{1,2,0:T(8,128)(2,1)}), bf16[4,256,1024]{1,2,0:T(8,128)(2,1)S(1)}, u32[]{:S(2)}, u32[]{:S(2)}) async-start(bf16[4,256,1024]{1,2,0:T(8,128)(2,1)} %bitcast.83), calls=%async_computation.1 | async-start | bytes 4194304 | tf_op jit(solution)/shard_map/all_to_all | solution.py:20
  52.8 350.8 %all-gather.5.cloned.1.call-start = ((), (), s32[]{:S(2)}) async-start(), calls=%async_computation.3 | async-start | bytes 10485760 | tf_op jit(solution)/shard_map/all_gather | solution.py:174
  52.8 202.0 %collective-permute-start.1 = (bf16[512,4096]{1,0:T(8,128)(2,1)}, bf16[512,4096]{1,0:T(8,128)(2,1)}, u32[]{:S(2)}, u32[]{:S(2)}) collective-permute-start(bf16[512,4096]{1,0:T(8,128)(2,1)} %param.13), channel_id=1, source_target_pairs={{0,4},{2,6},{4,0},{6,2},{8,12},{10,14},{12,8},{14,10},{16,20},{18,... | collective-permute-start | bytes 12582920 | tf_op jit(solution)/shard_map/ppermute | solution.py:28
  56.2 209.3 %collective-permute-start.2 = (bf16[512,4096]{1,0:T(8,128)(2,1)}, bf16[512,4096]{1,0:T(8,128)(2,1)}, u32[]{:S(2)}, u32[]{:S(2)}) collective-permute-start(bf16[512,4096]{1,0:T(8,128)(2,1)} %param.13), channel_id=1, source_target_pairs={{0,6},{2,4},{4,2},{6,0},{8,14},{10,12},{12,10},{14,8},{16,22},{18,... | collective-permute-start | bytes 12582920 | tf_op jit(solution)/shard_map/ppermute | solution.py:28
  230.2 9.8 %copy-start.12 = (bf16[4096,1296]{0,1:T(8,128)(2,1)S(1)}, bf16[4096,1296]{0,1:T(8,128)(2,1)}, u32[]{:S(2)}) copy-start(bf16[4096,1296]{0,1:T(8,128)(2,1)} %all-gather.3.cloned.1.call-done) | copy-start | bytes 31850500
  287.7 1.3 copy-start.5
  287.7 1.7 copy-start.4
  289.9 2.3 copy-start.2
  289.9 5.1 %collective-permute-start.3 = (bf16[3,1280]{1,0:T(4,128)(2,1)S(1)}, bf16[3,1280]{1,0:T(4,128)(2,1)S(1)}, u32[]{:S(2)}, u32[]{:S(2)}) collective-permute-start(bf16[3,1280]{1,0:T(4,128)(2,1)S(1)} %slice.126), channel_id=1, source_target_pairs={{0,8},{2,10},{4,12},{6,14},{8,16},{10,18},{12,20},{14,22},{16,24},... | collective-permute-start | bytes 23048 | tf_op jit(solution)/shard_map/ppermute | solution.py:187
  324.2 22.4 %collective-permute-start.4 = (bf16[130,1024]{1,0:T(8,128)(2,1)S(1)}, bf16[130,1024]{1,0:T(8,128)(2,1)S(1)}, u32[]{:S(2)}, u32[]{:S(2)}) collective-permute-start(bf16[130,1024]{1,0:T(8,128)(2,1)S(1)} %pad_maximum_fusion.1), channel_id=1, source_target_pairs={{0,8},{2,10},{4,12},{6,14},{8,16},{10,18},{12,20},{14,22},{16,24},... | collective-permute-start | bytes 798728 | tf_op jit(solution)/shard_map/ppermute | solution.py:35
  325.5 49.7 %collective-permute-start.5 = (bf16[130,1024]{1,0:T(8,128)(2,1)S(1)}, bf16[130,1024]{1,0:T(8,128)(2,1)S(1)}, u32[]{:S(2)}, u32[]{:S(2)}) collective-permute-start(bf16[130,1024]{1,0:T(8,128)(2,1)S(1)} %pad_maximum_fusion.1), channel_id=1, source_target_pairs={{0,16},{2,18},{4,20},{6,22},{8,24},{10,26},{12,28},{14,30},{1,17},... | collective-permute-start | bytes 798728 | tf_op jit(solution)/shard_map/ppermute | solution.py:35
  326.8 48.5 %collective-permute-start.6 = (bf16[130,1024]{1,0:T(8,128)(2,1)S(1)}, bf16[130,1024]{1,0:T(8,128)(2,1)S(1)}, u32[]{:S(2)}, u32[]{:S(2)}) collective-permute-start(bf16[130,1024]{1,0:T(8,128)(2,1)S(1)} %pad_maximum_fusion.1), channel_id=1, source_target_pairs={{0,24},{2,26},{4,28},{6,30},{1,25},{3,27},{5,29},{7,31}} | collective-permute-start | bytes 798728 | tf_op jit(solution)/shard_map/ppermute | solution.py:35
  403.6 10.2 %copy-start.3 = (f32[2048,1024]{1,0:T(8,128)S(1)}, f32[2048,1024]{1,0:T(8,128)}, u32[]{:S(2)}) copy-start(f32[2048,1024]{1,0:T(8,128)} %multiply_add_fusion) | copy-start | bytes 25165828
  403.6 10.2 %copy-start.13 = (bf16[4096,1024]{1,0:T(8,128)(2,1)S(1)}, bf16[4096,1024]{1,0:T(8,128)(2,1)}, u32[]{:S(2)}) copy-start(bf16[4096,1024]{1,0:T(8,128)(2,1)} %all-gather.5.cloned.1.call-done) | copy-start | bytes 25165828
  427.8 3.3 copy-start.14
  428.5 25.3 %collective-permute-start.7 = (bf16[512,1024]{1,0:T(8,128)(2,1)S(1)}, bf16[512,1024]{1,0:T(8,128)(2,1)S(1)}, u32[]{:S(2)}, u32[]{:S(2)}) collective-permute-start(bf16[512,1024]{1,0:T(8,128)(2,1)S(1)} %get-tuple-element.33), channel_id=1, source_target_pairs={{0,6},{2,4},{4,2},{6,0},{8,14},{10,12},{12,10},{14,8},{16,22},{18,... | collective-permute-start | bytes 3145736 | tf_op jit(solution)/shard_map/ppermute | solution.py:28
  429.7 47.3 %collective-permute-start.8 = (bf16[512,1024]{1,0:T(8,128)(2,1)S(1)}, bf16[512,1024]{1,0:T(8,128)(2,1)S(1)}, u32[]{:S(2)}, u32[]{:S(2)}) collective-permute-start(bf16[512,1024]{1,0:T(8,128)(2,1)S(1)} %get-tuple-element.32), channel_id=1, source_target_pairs={{0,4},{2,6},{4,0},{6,2},{8,12},{10,14},{12,8},{14,10},{16,20},{18,... | collective-permute-start | bytes 3145736 | tf_op jit(solution)/shard_map/ppermute | solution.py:28
  430.0 47.1 %collective-permute-start.9 = (bf16[512,1024]{1,0:T(8,128)(2,1)S(1)}, bf16[512,1024]{1,0:T(8,128)(2,1)S(1)}, u32[]{:S(2)}, u32[]{:S(2)}) collective-permute-start(bf16[512,1024]{1,0:T(8,128)(2,1)S(1)} %get-tuple-element.31), channel_id=1, source_target_pairs={{0,2},{2,0},{4,6},{6,4},{8,10},{10,8},{12,14},{14,12},{16,18},{18,... | collective-permute-start | bytes 3145736 | tf_op jit(solution)/shard_map/ppermute | solution.py:28
  454.3 26.2 %copy-start.1 = (f32[4,4096]{1,0:T(4,128)S(1)}, f32[4,4096]{1,0:T(4,128)}, u32[]{:S(2)}) copy-start(f32[4,4096]{1,0:T(4,128)} %param.18) | copy-start | bytes 196612
  477.2 2.0 copy-start.6
Sparse Core Ops, SparseCore 0:
  45.3 184.8 all-gather.2
  231.8 171.7 all-gather.4

commit v4 on v3

--- a/solution.py
+++ b/solution.py
@@ -26,6 +26,18 @@
 def swapped(value, step, plane):
     pairs = [(i, i - i % plane + (i % plane ^ step)) for i in range(lax.axis_size("ctx"))]
     return lax.ppermute(value, "ctx", pairs)
+
+
+def shared(value, step, plane):
+    if lax.axis_size("grp") != 2:
+        return swapped(value, step, plane)
+    core = lax.axis_index("grp")
+    half = value.shape[0] // 2
+    got = swapped(lax.dynamic_slice_in_dim(value, core * half, half), step, plane)
+    other = lax.ppermute(got, "grp", [(0, 1), (1, 0)])
+    lower = jnp.where(core == 0, got, other)
+    upper = jnp.where(core == 0, other, got)
+    return jnp.concatenate([lower, upper])
 
 
 def earlier_parts(value, along, plane, depth):
@@ -169,7 +181,7 @@
     main = exchange_columns(main, in_plane, plane)
     main, tokens, w_z = lax.optimization_barrier((main, tokens, w_z))
     main = lax.all_gather(main, "ctx", axis=0, tiled=True, axis_index_groups=along)
-    pieces = [tokens] + [swapped(tokens, step, plane) for step in range(1, plane)]
+    pieces = [tokens] + [shared(tokens, step, plane) for step in range(1, plane)]
     w_gate = exchange_columns(w_z, in_plane, plane)
     w_gate = lax.all_gather(w_gate, "ctx", axis=0, tiled=True, axis_index_groups=along)
     rows = own_rows * plane

time: 497 us -> 494 us (level)
  waiting for transfers between devices: 275 us -> 218 us
  starting transfers between devices: 14.7 us -> 59.1 us
  other arithmetic: 27.4 us -> 40.5 us
    all_to_all x1, waiting for transfers between devices: 102 us -> 18.9 us  [exchange_columns(): lax.all_to_all(parts.swapaxes(0, 1), 'ctx', 0, 0, axis_index_groups=group...]
    ppermute x0 -> x3, starting transfers between devices: none -> 43.4 us  [shared(): other = lax.ppermute(got, 'grp', [(0, 1), (1, 0)])]
    ppermute x6, waiting for transfers between devices: 45.6 us -> 80.4 us  [swapped(): return lax.ppermute(value, 'ctx', pairs)]
    all_gather x1, waiting for transfers between devices: 69.1 us -> 49.2 us  [on_device(): lax.all_gather(main, 'ctx', axis=0, tiled=True, axis_index_groups=along)]
    select_n x0 -> x3, other arithmetic: none -> 13 us  [shared(): lower = jnp.where(core == 0, got, other)]
    dot_general x4, matrix products: 37.5 us -> 30.1 us  [on_device(): projected = jnp.dot(piece, main, preferred_element_type=F32)]
    ppermute x3, waiting for transfers between devices: 39.8 us -> 46.2 us  [earlier_parts(): yield lax.ppermute(value, 'ctx', pairs)]
    all_gather x1, waiting for transfers between devices: 16.4 us -> 21.5 us  [on_device(): lax.all_gather(w_gate, 'ctx', axis=0, tiled=True, axis_index_groups=along)]
  transfers between devices with their start and end apart: 13 -> 16, of which waited for: 9 -> 9; matrix products, arithmetic and copies ran while one was open for 20% -> 22% of each run, Pallas kernels for 3% -> 3%
where the time goes in v4:
time: 494 us; the launch traced here: 489 us
  waiting for transfers between devices  218 us (44%)
  matrix products  74.2 us (15%)
  starting transfers between devices  59.1 us (12%)
  other arithmetic  40.5 us (8%)
  local copies, waits for them, and re-layouts  33.1 us (7%)
  blocking collectives  32.9 us (7%)
  Pallas kernels  16.7 us (3%)
  between operations  14.4 us (3%)
    ppermute x6, waiting for transfers between devices, swapped(): return lax.ppermute(value, 'ctx', pairs)  80.4 us
    all_gather x1, waiting for transfers between devices, on_device(): lax.all_gather(main, 'ctx', axis=0, tiled=True, axis_index_groups=along)  49.2 us
    ppermute x3, waiting for transfers between devices, earlier_parts(): yield lax.ppermute(value, 'ctx', pairs)  46.2 us
    ppermute x3, starting transfers between devices, shared(): other = lax.ppermute(got, 'grp', [(0, 1), (1, 0)])  43.4 us
    all_to_all x1, blocking collectives, exchange_columns(): lax.all_to_all(parts.swapaxes(0, 1), 'ctx', 0, 0, axis_index_groups=group...  32.9 us
    dot_general x4, matrix products, on_device(): jnp.dot(pieces[step], w_gate, preferred_element_type=F32).astype(BF16)  32.8 us
    dot_general x4, matrix products, on_device(): projected = jnp.dot(piece, main, preferred_element_type=F32)  30.1 us
    all_gather x1, waiting for transfers between devices, on_device(): lax.all_gather(w_gate, 'ctx', axis=0, tiled=True, axis_index_groups=along)  21.5 us
  transfers between devices with their start and end apart: 16, of which 9 were waited for; matrix products, arithmetic and copies ran while one was open for 22% of the time, Pallas kernels for 3%

profile of v4, /device:TPU:27, one launch (start us, length us, event | category | flops | bytes accessed | tf_op | source)
XLA Modules:
  0.0 488.6 jit_solution(8705768128640493001)
XLA Ops:
  6.5 3.3 copy.83
  10.4 32.9 %all_to_all.10 = bf16[4,256,1296]{1,2,0:T(8,128)(2,1)S(1)} all-to-all(bf16[4,256,1296]{1,2,0:T(8,128)(2,1)S(1)} %maximum_bitcast_fusion), channel_id=1, replica_groups={{0,2,4,6},{8,10,12,14},{16,18,20,22},{24,26,28,30},{1,3,5,7},{9,11,13,1..., dimensions={0} | all-to-all | bytes 5308416 | tf_op jit(solution)/shard_map/all_to_all | solution.py:20
  45.2 3.3 constant_dynamic-slice_fusion
  51.2 42.7 %collective-permute-done = bf16[256,4096]{1,0:T(8,128)(2,1)} collective-permute-done((bf16[256,4096]{1,0:T(8,128)(2,1)}, bf16[256,4096]{1,0:T(8,128)(2,1)}, u32[]{:S(2)}, u32[]{:S(2)}) %collective-permute-start) | collective-permute-done | bytes 2097184 | tf_op jit(solution)/shard_map/ppermute | solution.py:28
  93.9 5.6 %collective-permute-start.1 = (bf16[256,4096]{1,0:T(8,128)(2,1)}, bf16[256,4096]{1,0:T(8,128)(2,1)}, u32[]{:S(2)}, u32[]{:S(2)}) collective-permute-start(bf16[256,4096]{1,0:T(8,128)(2,1)} %collective-permute-done), channel_id=1, source_target_pairs={{0,1},{1,0},{2,3},{3,2},{4,5},{5,4},{6,7},{7,6},{8,9},{9,8},{10,11... | collective-permute-start | bytes 6291464 | tf_op jit(solution)/shard_map/ppermute | solution.py:37
  102.0 4.7 all-to-all-start.1
  106.7 36.6 %collective-permute-start.3 = (bf16[256,4096]{1,0:T(8,128)(2,1)}, bf16[256,4096]{1,0:T(8,128)(2,1)}, u32[]{:S(2)}, u32[]{:S(2)}) collective-permute-start(bf16[256,4096]{1,0:T(8,128)(2,1)} %collective-permute-done.2), channel_id=1, source_target_pairs={{0,1},{1,0},{2,3},{3,2},{4,5},{5,4},{6,7},{7,6},{8,9},{9,8},{10,11... | collective-permute-start | bytes 6291464 | tf_op jit(solution)/shard_map/ppermute | solution.py:37
  145.5 18.9 %all-to-all-done.1 = bf16[4,256,1024]{1,2,0:T(8,128)(2,1)S(1)} async-done(((bf16[4,256,1024]{1,2,0:T(8,128)(2,1)}), bf16[4,256,1024]{1,2,0:T(8,128)(2,1)S(1)}, u32[]{:S(2)}, u32[]{:S(2)}) %all-to-all-start.1) | async-done | bytes 2097184 | tf_op jit(solution)/shard_map/all_to_all | solution.py:20
  164.4 2.5 copy.103
  168.1 3.9 broadcast_select_fusion.5
  171.9 5.3 %broadcast_select_fusion.3 = (bf16[256,4096]{1,0:T(8,128)(2,1)}, bf16[256,4096]{1,0:T(8,128)(2,1)}) fusion(bf16[256,4096]{1,0:T(8,128)(2,1)} %collective-permute-done.2, bf16[256,4096]{1,0:T(8,128)(2,1)} %collective-permute-done.3, pred[]{:T(512)S(6)} %eq.6), kind=kLoop, calls=%fused_computation.56 | loop fusion | flops 2097152 | bytes 8388609 | tf_op jit(solution)/shard_map/jit(_where)/select_n | solution.py:38
  177.2 3.8 broadcast_select_fusion.1
  181.0 49.2 %all-gather.3.cloned.1.call-done = bf16[4096,1296]{0,1:T(8,128)(2,1)} async-done(((bf16[1024,1296]{0,1:T(8,128)(2,1)}), bf16[4096,1296]{0,1:T(8,128)(2,1)}) %all-gather.3.cloned.1.call-update) | async-done | bytes 10616848 | tf_op jit(solution)/shard_map/all_gather | solution.py:183
  230.2 10.0 %fusion.57 = f32[512,1296]{0,1:T(8,128)S(1)} fusion(bf16[512,4096]{1,0:T(8,128)(2,1)} %param.13, bf16[4096,1296]{0,1:T(8,128)(2,1)} %all-gather.3.cloned.1.call-done), kind=kOutput, calls=%fused_computation.139 | convolution fusion | flops 5435817984 | bytes 17465344 | tf_op jit(solution)/shard_map/dot_general | solution.py:193
  240.3 5.7 %fusion.7 = f32[512,1296]{0,1:T(8,128)S(1)} fusion(bf16[4096,1296]{0,1:T(8,128)(2,1)S(1)} %copy-done.23, bf16[256,4096]{1,0:T(8,128)(2,1)S(1)} %copy-done.10, bf16[256,4096]{1,0:T(8,128)(2,1)S(1)} %get-tuple-element.29), kind=kOutput, calls=%fused_computation.15 | convolution fusion | flops 5444206592 | bytes 17465344 | tf_op jit(solution)/shard_map/dot_general | solution.py:193
  246.0 5.7 %fusion.5 = f32[512,1296]{0,1:T(8,128)S(1)} fusion(bf16[4096,1296]{0,1:T(8,128)(2,1)S(1)} %copy-done.23, bf16[256,4096]{1,0:T(8,128)(2,1)S(1)} %copy-done.14, bf16[256,4096]{1,0:T(8,128)(2,1)S(1)} %copy-done.12), kind=kOutput, calls=%fused_computation.13 | convolution fusion | flops 5444206592 | bytes 17465344 | tf_op jit(solution)/shard_map/dot_general | solution.py:193
  254.5 8.6 %fusion.3 = f32[512,1296]{0,1:T(8,128)S(1)} fusion(bf16[4096,1296]{0,1:T(8,128)(2,1)} %all-gather.3.cloned.1.call-done, bf16[256,4096]{1,0:T(8,128)(2,1)S(1)} %copy-done.17, bf16[256,4096]{1,0:T(8,128)(2,1)S(1)} %copy-done.16), kind=kOutput, calls=%fused_computation.11 | convolution fusion | flops 5444206592 | bytes 17465344 | tf_op jit(solution)/shard_map/dot_general | solution.py:193
  264.6 4.6 reduce-window.6
  283.2 12.6 %multiply_convert_fusion.conv = bf16[2048,1280]{1,0:T(8,128)(2,1)S(1)} fusion(bf16[2048,1280]{1,0:T(8,128)(2,1)} %copy-done.2, bf16[3,1280]{1,0:T(4,128)(2,1)S(1)} %collective-permute-done.6, f32[1280]{0:T(1024)S(1)} %get-tuple-element.21, f32[1280]{0:T(1024)S(1)} %get-tuple-element.22, f32[1280]{0:T(1024)S(1)} %get-tuple-element.20, ...), kind=kLoop, calls=%fused_computation | loop fusion | flops 68157440 | bytes 10519040 | tf_op jit(solution)/shard_map/convert_element_type | solution.py:210
  295.8 16.7 %local_scan.1 = (f32[2048,1024]{1,0:T(8,128)S(1)}, f32[128,1024]{1,0:T(8,128)S(1)}) custom-call(bf16[2048,1280]{1,0:T(8,128)(2,1)S(1)} %multiply_convert_fusion.conv, f32[2048,16]{1,0:T(8,128)S(1)} %bitcast.71, f32[8,16,256]{2,1,0:T(8,128)S(1)} %get-tuple-element.35.cumul_t, f32[8,16,256]{2,1,0:T(8,128)S(1)} %bitcast.73, f32[2048,16]{1,0:T(8,128)S(1)} %bitcast.72, ...), custom_call_target="tpu_custom_call" | custom-call | flops 2147483648 | bytes 16777216 | tf_op jit(solution)/shard_map/local_scan/pallas_call | solution.py:107
  316.9 6.8 %fusion.58 = f32[2048,1024]{1,0:T(8,128)S(1)} fusion(f32[2048,16]{0,1:T(8,128)S(1)} %bitcast.81, f32[16,1024]{1,0:T(8,128)S(1)} %reshape.103), kind=kOutput, calls=%fused_computation.140 | convolution fusion | flops 402653184 | bytes 8585216 | tf_op jit(solution)/shard_map/dot_general | solution.py:233
  323.7 10.5 %collective-permute-done.7 = bf16[130,1024]{1,0:T(8,128)(2,1)S(1)} collective-permute-done((bf16[130,1024]{1,0:T(8,128)(2,1)S(1)}, bf16[130,1024]{1,0:T(8,128)(2,1)S(1)}, u32[]{:S(2)}, u32[]{:S(2)}) %collective-permute-start.7) | collective-permute-done | bytes 266272 | tf_op jit(solution)/shard_map/ppermute | solution.py:47
  334.3 35.7 %collective-permute-done.8 = bf16[130,1024]{1,0:T(8,128)(2,1)S(1)} collective-permute-done((bf16[130,1024]{1,0:T(8,128)(2,1)S(1)}, bf16[130,1024]{1,0:T(8,128)(2,1)S(1)}, u32[]{:S(2)}, u32[]{:S(2)}) %collective-permute-start.8) | collective-permute-done | bytes 266272 | tf_op jit(solution)/shard_map/ppermute | solution.py:47
  370.1 4.5 fusion.31
  374.7 7.4 %multiply_add_fusion = f32[2048,1024]{1,0:T(8,128)} fusion(f32[2048,1024]{1,0:T(8,128)S(1)} %get-tuple-element.14, f32[2048,1024]{1,0:T(8,128)} %fusion.31, f32[2048,1024]{1,0:T(8,128)S(1)} %fusion.58), kind=kLoop, calls=%fused_computation.1 | loop fusion | flops 4194304 | bytes 33554432 | tf_op jit(solution)/shard_map/add | solution.py:253
  382.1 21.5 %all-gather.5.cloned.1.call-done = bf16[4096,1024]{1,0:T(8,128)(2,1)} async-done(((bf16[1024,1024]{1,0:T(8,128)(2,1)}), bf16[4096,1024]{1,0:T(8,128)(2,1)}) %all-gather.5.cloned.1.call-update) | async-done | bytes 8388624 | tf_op jit(solution)/shard_map/all_gather | solution.py:186
  403.6 10.3 %multiply_reduce_fusion.3 = (f32[512]{0:T(512)S(1)}, f32[512,1024]{1,0:T(8,128)S(1)}) fusion(bf16[4096,1024]{1,0:T(8,128)(2,1)} %all-gather.5.cloned.1.call-done, bf16[256,4096]{1,0:T(8,128)(2,1)} %get-tuple-element.26, bf16[256,4096]{1,0:T(8,128)(2,1)} %get-tuple-element.25, f32[2048,1024]{1,0:T(8,128)} %multiply_add_fusion, s32[]{:T(128)S(6)} %select_n.102), kind=kOutput, calls=%fused_computation.52 | convolution fusion | flops 4308073984 | bytes 16779268 | tf_op jit(solution)/shard_map/dot_general | solution.py:259
  413.9 7.6 %multiply_reduce_fusion.2 = (f32[512]{0:T(512)S(1)}, f32[512,1024]{1,0:T(8,128)S(1)}) fusion(bf16[4096,1024]{1,0:T(8,128)(2,1)} %all-gather.5.cloned.1.call-done, bf16[256,4096]{1,0:T(8,128)(2,1)S(1)} %copy-done.15, bf16[256,4096]{1,0:T(8,128)(2,1)S(1)} %copy-done.13, f32[2048,1024]{1,0:T(8,128)S(1)} %copy-done.3, s32[]{:T(128)S(6)} %select_n.99), kind=kOutput, calls=%fused_computation.50 | convolution fusion | flops 4308073984 | bytes 16779268 | tf_op jit(solution)/shard_map/dot_general | solution.py:259
  421.5 7.5 %multiply_reduce_fusion.1 = (f32[512]{0:T(512)S(1)}, f32[512,1024]{1,0:T(8,128)S(1)}) fusion(bf16[4096,1024]{1,0:T(8,128)(2,1)} %all-gather.5.cloned.1.call-done, bf16[256,4096]{1,0:T(8,128)(2,1)S(1)} %copy-done.11, bf16[256,4096]{1,0:T(8,128)(2,1)S(1)} %copy-done.9, f32[2048,1024]{1,0:T(8,128)S(1)} %copy-done.3, s32[]{:T(128)S(6)} %select_n.96), kind=kOutput, calls=%fused_computation.48 | convolution fusion | flops 4308073984 | bytes 16779268 | tf_op jit(solution)/shard_map/dot_general | solution.py:259
  432.3 7.5 %multiply_reduce_fusion = (f32[512]{0:T(512)S(1)}, f32[512,1024]{1,0:T(8,128)S(1)}) fusion(bf16[512,4096]{1,0:T(8,128)(2,1)S(1)} %copy-done.18, bf16[4096,1024]{1,0:T(8,128)(2,1)} %all-gather.5.cloned.1.call-done, f32[2048,1024]{1,0:T(8,128)S(1)} %copy-done.3, s32[]{:T(128)S(6)} %select_n.91), kind=kOutput, calls=%fused_computation.46 | convolution fusion | flops 4299685376 | bytes 16779268 | tf_op jit(solution)/shard_map/dot_general | solution.py:259
  439.8 15.1 %collective-permute-done.10 = bf16[512,1024]{1,0:T(8,128)(2,1)S(1)} collective-permute-done((bf16[512,1024]{1,0:T(8,128)(2,1)S(1)}, bf16[512,1024]{1,0:T(8,128)(2,1)S(1)}, u32[]{:S(2)}, u32[]{:S(2)}) %collective-permute-start.10) | collective-permute-done | bytes 1048608 | tf_op jit(solution)/shard_map/ppermute | solution.py:28
  455.5 22.6 %collective-permute-done.11 = bf16[512,1024]{1,0:T(8,128)(2,1)S(1)} collective-permute-done((bf16[512,1024]{1,0:T(8,128)(2,1)S(1)}, bf16[512,1024]{1,0:T(8,128)(2,1)S(1)}, u32[]{:S(2)}, u32[]{:S(2)}) %collective-permute-start.11) | collective-permute-done | bytes 1048608 | tf_op jit(solution)/shard_map/ppermute | solution.py:28
  (155 shorter events, 40.9 us)
Async XLA Ops:
  6.5 138.8 %copy-start = (f32[4,4096]{1,0:T(4,128)S(1)}, f32[4,4096]{1,0:T(4,128)}, u32[]{:S(2)}) copy-start(f32[4,4096]{1,0:T(4,128)} %param.18) | copy-start | bytes 196612
  6.5 223.7 %all-gather.3.cloned.1.call-start = ((), (), s32[]{:S(2)}) async-start(), calls=%async_computation.2 | async-start | bytes 13271040 | tf_op jit(solution)/shard_map/all_gather | solution.py:183
  45.2 54.4 %copy-start.7 = (bf16[256,4096]{1,0:T(8,128)(2,1)S(1)}, bf16[256,4096]{1,0:T(8,128)(2,1)}, u32[]{:S(2)}) copy-start(bf16[256,4096]{1,0:T(8,128)(2,1)} %param.14) | copy-start | bytes 6291460
  48.5 94.8 %copy-start.21 = (f32[4,4,256]{2,1,0:T(4,128)S(1)}, f32[4,4,256]{2,1,0:T(4,128)}, u32[]{:S(2)}) copy-start(f32[4,4,256]{2,1,0:T(4,128)} %param.19) | copy-start | bytes 49156
  48.5 94.8 %copy-start.22 = (f32[4,256]{1,0:T(4,128)S(1)}, f32[4,256]{1,0:T(4,128)}, u32[]{:S(2)}) copy-start(f32[4,256]{1,0:T(4,128)} %param.21) | copy-start | bytes 12292
  48.5 94.8 %copy-start.24 = (f32[64]{0:T(128)S(1)}, f32[64]{0:T(128)}, u32[]{:S(2)}) copy-start(f32[64]{0:T(128)} %param.22) | copy-start | bytes 772
  48.5 94.9 %copy-start.25 = (f32[64]{0:T(128)S(1)}, f32[64]{0:T(128)}, u32[]{:S(2)}) copy-start(f32[64]{0:T(128)} %param.24) | copy-start | bytes 772
  48.5 96.9 %copy-start.26 = (f32[64]{0:T(128)S(1)}, f32[64]{0:T(128)}, u32[]{:S(2)}) copy-start(f32[64]{0:T(128)} %param.23) | copy-start | bytes 772
  48.5 45.4 %collective-permute-start = (bf16[256,4096]{1,0:T(8,128)(2,1)}, bf16[256,4096]{1,0:T(8,128)(2,1)}, u32[]{:S(2)}, u32[]{:S(2)}) collective-permute-start(bf16[256,4096]{1,0:T(8,128)(2,1)} %constant_dynamic-slice_fusion), channel_id=1, source_target_pairs={{0,2},{2,0},{4,6},{6,4},{8,10},{10,8},{12,14},{14,12},{16,18},{18,... | collective-permute-start | bytes 6291464 | tf_op jit(solution)/shard_map/ppermute | solution.py:28
  49.8 56.9 %collective-permute-start.2 = (bf16[256,4096]{1,0:T(8,128)(2,1)}, bf16[256,4096]{1,0:T(8,128)(2,1)}, u32[]{:S(2)}, u32[]{:S(2)}) collective-permute-start(bf16[256,4096]{1,0:T(8,128)(2,1)} %constant_dynamic-slice_fusion), channel_id=1, source_target_pairs={{0,4},{2,6},{4,0},{6,2},{8,12},{10,14},{12,8},{14,10},{16,20},{18,... | collective-permute-start | bytes 6291464 | tf_op jit(solution)/shard_map/ppermute | solution.py:28
  50.3 116.6 %collective-permute-start.4 = (bf16[256,4096]{1,0:T(8,128)(2,1)}, bf16[256,4096]{1,0:T(8,128)(2,1)}, u32[]{:S(2)}, u32[]{:S(2)}) collective-permute-start(bf16[256,4096]{1,0:T(8,128)(2,1)} %constant_dynamic-slice_fusion), channel_id=1, source_target_pairs={{0,6},{2,4},{4,2},{6,0},{8,14},{10,12},{12,10},{14,8},{16,22},{18,... | collective-permute-start | bytes 6291464 | tf_op jit(solution)/shard_map/ppermute | solution.py:28
  93.9 74.1 %collective-permute-start.1 = (bf16[256,4096]{1,0:T(8,128)(2,1)}, bf16[256,4096]{1,0:T(8,128)(2,1)}, u32[]{:S(2)}, u32[]{:S(2)}) collective-permute-start(bf16[256,4096]{1,0:T(8,128)(2,1)} %collective-permute-done), channel_id=1, source_target_pairs={{0,1},{1,0},{2,3},{3,2},{4,5},{5,4},{6,7},{7,6},{8,9},{9,8},{10,11... | collective-permute-start | bytes 6291464 | tf_op jit(solution)/shard_map/ppermute | solution.py:37
  102.0 62.4 %all-to-all-start.1 = ((bf16[4,256,1024]{1,2,0:T(8,128)(2,1)}), bf16[4,256,1024]{1,2,0:T(8,128)(2,1)S(1)}, u32[]{:S(2)}, u32[]{:S(2)}) async-start(bf16[4,256,1024]{1,2,0:T(8,128)(2,1)} %bitcast.77), calls=%async_computation.1 | async-start | bytes 4194304 | tf_op jit(solution)/shard_map/all_to_all | solution.py:20
  106.7 296.9 %all-gather.5.cloned.1.call-start = ((), (), s32[]{:S(2)}) async-start(), calls=%async_computation.3 | async-start | bytes 10485760 | tf_op jit(solution)/shard_map/all_gather | solution.py:186
  106.7 65.2 %collective-permute-start.3 = (bf16[256,4096]{1,0:T(8,128)(2,1)}, bf16[256,4096]{1,0:T(8,128)(2,1)}, u32[]{:S(2)}, u32[]{:S(2)}) collective-permute-start(bf16[256,4096]{1,0:T(8,128)(2,1)} %collective-permute-done.2), channel_id=1, source_target_pairs={{0,1},{1,0},{2,3},{3,2},{4,5},{5,4},{6,7},{7,6},{8,9},{9,8},{10,11... | collective-permute-start | bytes 6291464 | tf_op jit(solution)/shard_map/ppermute | solution.py:37
  166.9 10.3 %collective-permute-start.5 = (bf16[256,4096]{1,0:T(8,128)(2,1)}, bf16[256,4096]{1,0:T(8,128)(2,1)S(1)}, u32[]{:S(2)}, u32[]{:S(2)}) collective-permute-start(bf16[256,4096]{1,0:T(8,128)(2,1)} %collective-permute-done.4), channel_id=1, source_target_pairs={{0,1},{1,0},{2,3},{3,2},{4,5},{5,4},{6,7},{7,6},{8,9},{9,8},{10,11... | collective-permute-start | bytes 6291464 | tf_op jit(solution)/shard_map/ppermute | solution.py:37
  171.9 68.4 %copy-start.8 = (bf16[256,4096]{1,0:T(8,128)(2,1)}, bf16[256,4096]{1,0:T(8,128)(2,1)S(1)}, u32[]{:S(2)}) copy-start(bf16[256,4096]{1,0:T(8,128)(2,1)S(1)} %get-tuple-element.29) | copy-start | bytes 6291460
  230.2 10.1 %copy-start.10 = (bf16[256,4096]{1,0:T(8,128)(2,1)S(1)}, bf16[256,4096]{1,0:T(8,128)(2,1)}, u32[]{:S(2)}) copy-start(bf16[256,4096]{1,0:T(8,128)(2,1)} %get-tuple-element.30) | copy-start | bytes 6291460
  230.2 10.1 %copy-start.23 = (bf16[4096,1296]{0,1:T(8,128)(2,1)S(1)}, bf16[4096,1296]{0,1:T(8,128)(2,1)}, u32[]{:S(2)}) copy-start(bf16[4096,1296]{0,1:T(8,128)(2,1)} %all-gather.3.cloned.1.call-done) | copy-start | bytes 31850500
  278.2 5.0 %collective-permute-start.6 = (bf16[3,1280]{1,0:T(4,128)(2,1)S(1)}, bf16[3,1280]{1,0:T(4,128)(2,1)S(1)}, u32[]{:S(2)}, u32[]{:S(2)}) collective-permute-start(bf16[3,1280]{1,0:T(4,128)(2,1)S(1)} %slice.126), channel_id=1, source_target_pairs={{0,8},{2,10},{4,12},{6,14},{8,16},{10,18},{12,20},{14,22},{16,24},... | collective-permute-start | bytes 23048 | tf_op jit(solution)/shard_map/ppermute | solution.py:199
  312.5 21.7 %collective-permute-start.7 = (bf16[130,1024]{1,0:T(8,128)(2,1)S(1)}, bf16[130,1024]{1,0:T(8,128)(2,1)S(1)}, u32[]{:S(2)}, u32[]{:S(2)}) collective-permute-start(bf16[130,1024]{1,0:T(8,128)(2,1)S(1)} %pad_maximum_fusion.22), channel_id=1, source_target_pairs={{0,8},{2,10},{4,12},{6,14},{8,16},{10,18},{12,20},{14,22},{16,24},... | collective-permute-start | bytes 798728 | tf_op jit(solution)/shard_map/ppermute | solution.py:47
  313.8 56.2 %collective-permute-start.8 = (bf16[130,1024]{1,0:T(8,128)(2,1)S(1)}, bf16[130,1024]{1,0:T(8,128)(2,1)S(1)}, u32[]{:S(2)}, u32[]{:S(2)}) collective-permute-start(bf16[130,1024]{1,0:T(8,128)(2,1)S(1)} %pad_maximum_fusion.22), channel_id=1, source_target_pairs={{0,16},{2,18},{4,20},{6,22},{8,24},{10,26},{12,28},{14,30},{1,17},... | collective-permute-start | bytes 798728 | tf_op jit(solution)/shard_map/ppermute | solution.py:47
  315.1 55.0 %collective-permute-start.9 = (bf16[130,1024]{1,0:T(8,128)(2,1)S(1)}, bf16[130,1024]{1,0:T(8,128)(2,1)S(1)}, u32[]{:S(2)}, u32[]{:S(2)}) collective-permute-start(bf16[130,1024]{1,0:T(8,128)(2,1)S(1)} %pad_maximum_fusion.22), channel_id=1, source_target_pairs={{0,24},{2,26},{4,28},{6,30},{1,25},{3,27},{5,29},{7,31}} | collective-permute-start | bytes 798728 | tf_op jit(solution)/shard_map/ppermute | solution.py:47
  382.1 31.8 %copy-start.13 = (bf16[256,4096]{1,0:T(8,128)(2,1)S(1)}, bf16[256,4096]{1,0:T(8,128)(2,1)}, u32[]{:S(2)}) copy-start(bf16[256,4096]{1,0:T(8,128)(2,1)} %get-tuple-element.27) | copy-start | bytes 6291460
  403.6 10.3 %copy-start.3 = (f32[2048,1024]{1,0:T(8,128)S(1)}, f32[2048,1024]{1,0:T(8,128)}, u32[]{:S(2)}) copy-start(f32[2048,1024]{1,0:T(8,128)} %multiply_add_fusion) | copy-start | bytes 25165828
  403.6 10.3 %copy-start.15 = (bf16[256,4096]{1,0:T(8,128)(2,1)S(1)}, bf16[256,4096]{1,0:T(8,128)(2,1)}, u32[]{:S(2)}) copy-start(bf16[256,4096]{1,0:T(8,128)(2,1)} %get-tuple-element.28) | copy-start | bytes 6291460
  413.9 7.6 %copy-start.9 = (bf16[256,4096]{1,0:T(8,128)(2,1)S(1)}, bf16[256,4096]{1,0:T(8,128)(2,1)}, u32[]{:S(2)}) copy-start(bf16[256,4096]{1,0:T(8,128)(2,1)} %copy-done.8) | copy-start | bytes 6291460
  413.9 7.6 %copy-start.11 = (bf16[256,4096]{1,0:T(8,128)(2,1)S(1)}, bf16[256,4096]{1,0:T(8,128)(2,1)}, u32[]{:S(2)}) copy-start(bf16[256,4096]{1,0:T(8,128)(2,1)} %get-tuple-element.30) | copy-start | bytes 6291460
  429.6 25.3 %collective-permute-start.10 = (bf16[512,1024]{1,0:T(8,128)(2,1)S(1)}, bf16[512,1024]{1,0:T(8,128)(2,1)S(1)}, u32[]{:S(2)}, u32[]{:S(2)}) collective-permute-start(bf16[512,1024]{1,0:T(8,128)(2,1)S(1)} %get-tuple-element.39), channel_id=1, source_target_pairs={{0,6},{2,4},{4,2},{6,0},{8,14},{10,12},{12,10},{14,8},{16,22},{18,... | collective-permute-start | bytes 3145736 | tf_op jit(solution)/shard_map/ppermute | solution.py:28
  430.8 47.3 %collective-permute-start.11 = (bf16[512,1024]{1,0:T(8,128)(2,1)S(1)}, bf16[512,1024]{1,0:T(8,128)(2,1)S(1)}, u32[]{:S(2)}, u32[]{:S(2)}) collective-permute-start(bf16[512,1024]{1,0:T(8,128)(2,1)S(1)} %get-tuple-element.38), channel_id=1, source_target_pairs={{0,4},{2,6},{4,0},{6,2},{8,12},{10,14},{12,8},{14,10},{16,20},{18,... | collective-permute-start | bytes 3145736 | tf_op jit(solution)/shard_map/ppermute | solution.py:28
  430.9 47.3 %collective-permute-start.12 = (bf16[512,1024]{1,0:T(8,128)(2,1)S(1)}, bf16[512,1024]{1,0:T(8,128)(2,1)S(1)}, u32[]{:S(2)}, u32[]{:S(2)}) collective-permute-start(bf16[512,1024]{1,0:T(8,128)(2,1)S(1)} %get-tuple-element.37), channel_id=1, source_target_pairs={{0,2},{2,0},{4,6},{6,4},{8,10},{10,8},{12,14},{14,12},{16,18},{18,... | collective-permute-start | bytes 3145736 | tf_op jit(solution)/shard_map/ppermute | solution.py:28
  455.4 26.2 %copy-start.1 = (f32[4,4096]{1,0:T(4,128)S(1)}, f32[4,4096]{1,0:T(4,128)}, u32[]{:S(2)}) copy-start(f32[4,4096]{1,0:T(4,128)} %param.18) | copy-start | bytes 196612
  (11 other events, 34.0 us)
Sparse Core Ops, SparseCore 0:
  45.3 184.8 all-gather.2
  231.8 171.7 all-gather.4
